TPU v7x, 32 devices: a whole 2x2x4 slice. The times are simulated.
32 devices in a mesh: dp: 8 (over z, y), tensor: 4 (over x, core).
Axes of the slice: x: 2, y: 2, z: 4, core: 2. Of those that a mesh axis runs over, the one named last changes fastest.
Arguments:
- image_codes: int32 [32, 256], P('dp'), may hold values from 0 to 1023
- labels: int32 [32], P('dp'), may hold values from 0 to 999
- mask_flags: int32 [32, 256], P('dp'), may hold values from 0 to 1, as said below
- attend_in: float32 [2, 768, 3, 768], P(None, 'dp', None, 'tensor'), may hold values from -0.21875 to 0.21875
- attend_in_one: float32 [2, 768, 3, 768], P(None, 'dp', None, 'tensor'), may hold values from -3.33786e-06 to 3.33786e-06
- attend_in_two: float32 [2, 768, 3, 768], P(None, 'dp', None, 'tensor'), may hold values from 1.0048232e-12 to 4.0192927e-12
- attend_out: float32 [2, 768, 768], P(None, 'tensor', 'dp'), may hold values from -1.25 to 1.25
- attend_out_one: float32 [2, 768, 768], P(None, 'tensor', 'dp'), may hold values from -3.33786e-06 to 3.33786e-06
- attend_out_two: float32 [2, 768, 768], P(None, 'tensor', 'dp'), may hold values from 1.0048232e-12 to 4.0192927e-12
- expand: float32 [2, 768, 3072], P(None, 'dp', 'tensor'), may hold values from -0.21875 to 0.21875
- expand_one: float32 [2, 768, 3072], P(None, 'dp', 'tensor'), may hold values from -3.33786e-06 to 3.33786e-06
- expand_two: float32 [2, 768, 3072], P(None, 'dp', 'tensor'), may hold values from 1.0048232e-12 to 4.0192927e-12
- contract: float32 [2, 3072, 768], P(None, 'tensor', 'dp'), may hold values from -0.109375 to 0.109375
- contract_one: float32 [2, 3072, 768], P(None, 'tensor', 'dp'), may hold values from -3.33786e-06 to 3.33786e-06
- contract_two: float32 [2, 3072, 768], P(None, 'tensor', 'dp'), may hold values from 1.0048232e-12 to 4.0192927e-12
- embed_table: float32 [2304, 768], P('dp'), may hold values from -4.2 to 4.2
- embed_one: float32 [2304, 768], P('dp'), may hold values from -3.33786e-06 to 3.33786e-06
- embed_two: float32 [2304, 768], P('dp'), may hold values from 1.0048232e-12 to 4.0192927e-12
- logit_table: float32 [768, 1024], P('dp', 'tensor'), may hold values from -2 to 2
- logit_one: float32 [768, 1024], P('dp', 'tensor'), may hold values from -2.2888184e-05 to 2.2888184e-05
- logit_two: float32 [768, 1024], P('dp', 'tensor'), may hold values from 5.086263e-11 to 2.0345052e-10
- norm_params: float32 [5, 2, 768], P(None, None, 'dp'), may hold values from -0.8 to 2.4
- norm_one: float32 [5, 2, 768], P(None, None, 'dp'), may hold values from -1.335144e-05 to 1.335144e-05
- norm_two: float32 [5, 2, 768], P(None, None, 'dp'), may hold values from 1.6148943e-11 to 6.579199e-11
Outputs:
- new_attend_in: float32 [2, 768, 3, 768], P(None, 'dp', None, 'tensor')
- new_attend_in_one: float32 [2, 768, 3, 768], P(None, 'dp', None, 'tensor')
- new_attend_in_two: float32 [2, 768, 3, 768], P(None, 'dp', None, 'tensor')
- new_attend_out: float32 [2, 768, 768], P(None, 'tensor', 'dp')
- new_attend_out_one: float32 [2, 768, 768], P(None, 'tensor', 'dp')
- new_attend_out_two: float32 [2, 768, 768], P(None, 'tensor', 'dp')
- new_expand: float32 [2, 768, 3072], P(None, 'dp', 'tensor')
- new_expand_one: float32 [2, 768, 3072], P(None, 'dp', 'tensor')
- new_expand_two: float32 [2, 768, 3072], P(None, 'dp', 'tensor')
- new_contract: float32 [2, 3072, 768], P(None, 'tensor', 'dp')
- new_contract_one: float32 [2, 3072, 768], P(None, 'tensor', 'dp')
- new_contract_two: float32 [2, 3072, 768], P(None, 'tensor', 'dp')
- new_embed: float32 [2304, 768], P('dp')
- new_embed_one: float32 [2304, 768], P('dp')
- new_embed_two: float32 [2304, 768], P('dp')
- new_logit: float32 [768, 1024], P('dp', 'tensor')
- new_logit_one: float32 [768, 1024], P('dp', 'tensor')
- new_logit_two: float32 [768, 1024], P('dp', 'tensor')
- new_norm: float32 [5, 2, 768], P(None, None, 'dp')
- new_norm_one: float32 [5, 2, 768], P(None, None, 'dp')
- new_norm_two: float32 [5, 2, 768], P(None, None, 'dp')
- loss_sum: float32 [], replicated
- loss_count: float32 [], replicated
- grad_norm: float32 [], replicated
Inputs may be any that keep to these rules, and one draw needn't show every extreme that they name: `mask_flags`: every image has 1 to 256 masked positions, and in every draw some image has all 256 masked.
All inputs are finite; a program needn't handle non-finite values.
Results may differ from a plain program's by a relative error of at most 0.0044.
The roundings to bfloat16 on the way count: a program that leaves them out, or rounds other values in their place, can miss the bound.
Values may be sent and summed in bfloat16 or wider, within the bound.
A program may use at most 192 MiB of HBM per device.

v0:
```python
import jax
import jax.numpy as jnp
from jax import lax
from jax.sharding import PartitionSpec as P

HEADS = 16
CODES = 1024
CLASSES = 1000
LAYERS = 2
STEP = 10
SEQ = 257


beta_one = 0.9
beta_two = 0.96
matrix_rate = 0.02
embed_rate = 0.5
vector_rate = 0.25
weight_decay = 0.045
epsilon = 1e-10
clip_limit = 0.02
norm_epsilon = 1e-06


def layer_norm(stream, scaling, offset):
    average = jnp.mean(stream, axis=-1, keepdims=True)
    centred = stream - average
    variance = jnp.mean(centred * centred, axis=-1, keepdims=True)
    return centred * lax.rsqrt(variance + norm_epsilon) * scaling + offset


def norm_back(stream, scaling, offset, gradient):
    normed_out, pull = jax.vjp(layer_norm, stream, scaling, offset)
    return pull(gradient)


def gelu_exact(values):
    return jax.nn.gelu(values, approximate=False)


def matmul(left, right):
    return jnp.dot(left, right, preferred_element_type=jnp.float32)


def matmul_left(left, right):
    return lax.dot_general(
        left, right, (((0,), (0,)), ((), ())), preferred_element_type=jnp.float32
    )


def matmul_right(left, right):
    return lax.dot_general(
        left, right, (((1,), (1,)), ((), ())), preferred_element_type=jnp.float32
    )


def branch_total(piece_sum):
    return lax.psum(piece_sum.astype(jnp.bfloat16), "tensor").astype(jnp.float32)


def input_total(piece_sum):
    return lax.psum(piece_sum.astype(jnp.bfloat16), "tensor").astype(jnp.float32)


def split_heads(joined, images, head_count):
    head_width = joined.shape[1] // (3 * head_count)
    sections = joined.reshape(images, SEQ, 3, head_count, head_width)
    return (sections[:, :, 0], sections[:, :, 1], sections[:, :, 2], head_width ** (-0.5))


def attend_forward(joined, images, head_count):
    queries, key_rows, values, score_scale = split_heads(joined, images, head_count)
    scores = (
        jnp.einsum("bqhd,bkhd->bhqk", queries, key_rows, preferred_element_type=jnp.float32)
        * score_scale
    )
    peak_value = jnp.max(scores, axis=-1, keepdims=True)
    log_total = peak_value + jnp.log(jnp.sum(jnp.exp(scores - peak_value), axis=-1, keepdims=True))
    attention = jnp.exp(scores - log_total).astype(jnp.bfloat16)
    blended = jnp.einsum("bhqk,bkhd->bqhd", attention, values, preferred_element_type=jnp.float32)
    return (blended.astype(jnp.bfloat16).reshape(joined.shape[0], -1), log_total)


def attend_backward(joined, log_total, grad_blended, images, head_count):
    queries, key_rows, values, score_scale = split_heads(joined, images, head_count)
    scores = (
        jnp.einsum("bqhd,bkhd->bhqk", queries, key_rows, preferred_element_type=jnp.float32)
        * score_scale
    )
    attention = jnp.exp(scores - log_total)
    grad_out = grad_blended.reshape(queries.shape)
    grad_attention = jnp.einsum(
        "bqhd,bkhd->bhqk", grad_out, values, preferred_element_type=jnp.float32
    )
    row_total = jnp.sum(attention * grad_attention, axis=-1, keepdims=True)
    grad_scores = (attention * (grad_attention - row_total)).astype(jnp.bfloat16)
    grad_queries = (
        jnp.einsum("bhqk,bkhd->bqhd", grad_scores, key_rows, preferred_element_type=jnp.float32)
        * score_scale
    )
    grad_keys = (
        jnp.einsum("bhqk,bqhd->bkhd", grad_scores, queries, preferred_element_type=jnp.float32)
        * score_scale
    )
    grad_values = jnp.einsum(
        "bhqk,bqhd->bkhd",
        attention.astype(jnp.bfloat16),
        grad_out,
        preferred_element_type=jnp.float32,
    )
    stacked = jnp.stack([grad_queries, grad_keys, grad_values], axis=2).astype(jnp.bfloat16)
    return stacked.reshape(joined.shape)


def layer_forward(stream, weights, gains, images, head_count):
    w_in, w_out, w_expand, w_contract = weights
    normed = layer_norm(stream, gains[0, 0], gains[0, 1]).astype(jnp.bfloat16)
    joined = matmul(normed, w_in.reshape(w_in.shape[0], -1)).astype(jnp.bfloat16)
    blended, log_total = attend_forward(joined, images, head_count)
    middle = stream + branch_total(matmul(blended, w_out))
    normed_two = layer_norm(middle, gains[1, 0], gains[1, 1]).astype(jnp.bfloat16)
    hidden = matmul(normed_two, w_expand)
    active = gelu_exact(hidden).astype(jnp.bfloat16)
    result = middle + branch_total(matmul(active, w_contract))
    return (
        result,
        (stream, normed, joined, blended, log_total, middle, normed_two, hidden, active),
    )


def layer_backward(gradient, saved, weights, gains, images, head_count):
    w_in, w_out, w_expand, w_contract = weights
    stream, normed, joined, blended, log_total, middle, normed_two, hidden, active = saved
    grad_low = gradient.astype(jnp.bfloat16)
    g_contract = matmul_left(active, grad_low)
    grad_active = matmul_right(grad_low, w_contract)
    gelu_out, gelu_pull = jax.vjp(gelu_exact, hidden)
    grad_hidden = gelu_pull(grad_active)[0].astype(jnp.bfloat16)
    g_expand = matmul_left(normed_two, grad_hidden)
    grad_normed = input_total(matmul_right(grad_hidden, w_expand))
    grad_mid, scale_two, offset_two = norm_back(middle, gains[1, 0], gains[1, 1], grad_normed)
    gradient = gradient + grad_mid
    grad_low = gradient.astype(jnp.bfloat16)
    g_out = matmul_left(blended, grad_low)
    grad_blended = matmul_right(grad_low, w_out).astype(jnp.bfloat16)
    grad_joined = attend_backward(joined, log_total, grad_blended, images, head_count)
    g_in = matmul_left(normed, grad_joined).reshape(w_in.shape)
    grad_normed = input_total(matmul_right(grad_joined, w_in.reshape(w_in.shape[0], -1)))
    grad_first, scale_one, offset_one = norm_back(stream, gains[0, 0], gains[0, 1], grad_normed)
    norm_grads = jnp.stack([jnp.stack([scale_one, offset_one]), jnp.stack([scale_two, offset_two])])
    return (gradient + grad_first, (g_in, g_out, g_expand, g_contract), norm_grads)


def adam_step(weight, moment_one, moment_two, gradient, factor, rate_here, decay_here):
    gradient = gradient * factor
    moment_one = beta_one * moment_one + (1.0 - beta_one) * gradient
    moment_two = beta_two * moment_two + (1.0 - beta_two) * gradient * gradient
    correct_one = 1.0 - beta_one**STEP
    correct_two = 1.0 - beta_two**STEP
    weight = weight - rate_here * (
        moment_one / correct_one / (jnp.sqrt(moment_two / correct_two) + epsilon)
        + decay_here * weight
    )
    return [weight, moment_one, moment_two]


def body(
    image_codes,
    labels,
    mask_flags,
    attend_in,
    attend_in_one,
    attend_in_two,
    attend_out,
    attend_out_one,
    attend_out_two,
    expand,
    expand_one,
    expand_two,
    contract,
    contract_one,
    contract_two,
    embed_table,
    embed_one,
    embed_two,
    logit_table,
    logit_one,
    logit_two,
    norm_params,
    norm_one,
    norm_two,
):
    w_in, w_out, w_expand, w_contract, embed_rows, head_table, gains_low = (
        lax.all_gather(attend_in.astype(jnp.bfloat16), "dp", axis=1, tiled=True),
        lax.all_gather(attend_out.astype(jnp.bfloat16), "dp", axis=2, tiled=True),
        lax.all_gather(expand.astype(jnp.bfloat16), "dp", axis=1, tiled=True),
        lax.all_gather(contract.astype(jnp.bfloat16), "dp", axis=2, tiled=True),
        lax.all_gather(embed_table.astype(jnp.bfloat16), "dp", axis=0, tiled=True),
        lax.all_gather(logit_table.astype(jnp.bfloat16), "dp", axis=0, tiled=True),
        lax.all_gather(norm_params.astype(jnp.bfloat16), "dp", axis=2, tiled=True),
    )
    gains = gains_low.astype(jnp.float32)
    images = labels.shape[0]
    head_count = HEADS // lax.axis_size("tensor")
    code_rows = jnp.where(mask_flags == 1, CODES, image_codes)
    row_index = jnp.concatenate([(CODES + 1 + labels)[:, None], code_rows], axis=1).reshape(-1)
    place_rows = jnp.tile(CODES + 1 + CLASSES + jnp.arange(SEQ), images)
    targets = jnp.concatenate([jnp.zeros((images, 1), jnp.int32), image_codes], axis=1).reshape(-1)
    weights_loss = jnp.concatenate(
        [jnp.zeros((images, 1), jnp.float32), mask_flags.astype(jnp.float32)], axis=1
    ).reshape(-1)
    stream = embed_rows[row_index].astype(jnp.float32) + embed_rows[place_rows].astype(jnp.float32)
    saved_all = []
    for layer_index in range(LAYERS):
        weights = (
            w_in[layer_index],
            w_out[layer_index],
            w_expand[layer_index],
            w_contract[layer_index],
        )
        stream, saved = layer_forward(
            stream, weights, gains[2 * layer_index : 2 * layer_index + 2], images, head_count
        )
        saved_all.append(saved)
    final_gain = gains[2 * LAYERS]
    final = layer_norm(stream, final_gain[0], final_gain[1]).astype(jnp.bfloat16)
    logits = matmul(final, head_table)
    local_codes = logits.shape[1]
    col_start = lax.axis_index("tensor") * local_codes
    is_target = (
        targets[:, None] == col_start + jnp.arange(local_codes, dtype=jnp.int32)[None, :]
    ).astype(jnp.float32)
    peak_value = jnp.max(logits, axis=1)
    exp_total = jnp.sum(jnp.exp(logits - peak_value[:, None]), axis=1)
    picked = jnp.sum(is_target * logits, axis=1)
    peak_all = lax.pmax(peak_value, "tensor")
    exp_all, picked_all = lax.psum((exp_total * jnp.exp(peak_value - peak_all), picked), "tensor")
    log_total = peak_all + jnp.log(exp_all)
    loss_terms = (log_total - picked_all) * weights_loss
    loss_sum, token_count = lax.psum((jnp.sum(loss_terms), jnp.sum(weights_loss)), "dp")
    grad_logits = (
        (jnp.exp(logits - log_total[:, None]) - is_target) * (weights_loss / token_count)[:, None]
    ).astype(jnp.bfloat16)
    g_head = matmul_left(final, grad_logits)
    grad_final = input_total(matmul_right(grad_logits, head_table))
    gradient, final_scale, final_offset = norm_back(
        stream, final_gain[0], final_gain[1], grad_final
    )
    layer_grads = [None] * LAYERS
    norm_grads = [None] * LAYERS
    for layer_index in reversed(range(LAYERS)):
        weights = (
            w_in[layer_index],
            w_out[layer_index],
            w_expand[layer_index],
            w_contract[layer_index],
        )
        gradient, found, gain_grads = layer_backward(
            gradient,
            saved_all[layer_index],
            weights,
            gains[2 * layer_index : 2 * layer_index + 2],
            images,
            head_count,
        )
        layer_grads[layer_index] = found
        norm_grads[layer_index] = gain_grads
    g_norms = jnp.concatenate(
        [
            jnp.stack(norm_grads).reshape(2 * LAYERS, 2, -1),
            jnp.stack([final_scale, final_offset])[None],
        ],
        axis=0,
    )
    g_table = jax.ops.segment_sum(
        jnp.concatenate([gradient, gradient], axis=0),
        jnp.concatenate([row_index, place_rows]),
        num_segments=embed_rows.shape[0],
    )
    g_in_all = jnp.stack([found[0] for found in layer_grads])
    g_out_all = jnp.stack([found[1] for found in layer_grads])
    g_expand_all = jnp.stack([found[2] for found in layer_grads])
    g_contract_all = jnp.stack([found[3] for found in layer_grads])
    g_in_all, g_out_all, g_expand_all, g_contract_all, g_table, g_head, g_norms = (
        lax.psum_scatter(g_in_all, "dp", scatter_dimension=1, tiled=True),
        lax.psum_scatter(g_out_all, "dp", scatter_dimension=2, tiled=True),
        lax.psum_scatter(g_expand_all, "dp", scatter_dimension=1, tiled=True),
        lax.psum_scatter(g_contract_all, "dp", scatter_dimension=2, tiled=True),
        lax.psum_scatter(g_table, "dp", scatter_dimension=0, tiled=True),
        lax.psum_scatter(g_head, "dp", scatter_dimension=0, tiled=True),
        lax.psum_scatter(g_norms, "dp", scatter_dimension=2, tiled=True),
    )
    gradients = (g_in_all, g_out_all, g_expand_all, g_contract_all, g_table, g_head, g_norms)
    first_rank = (lax.axis_index("tensor") == 0).astype(jnp.float32)
    split_squares = (
        jnp.sum(g_in_all * g_in_all)
        + jnp.sum(g_out_all * g_out_all)
        + jnp.sum(g_expand_all * g_expand_all)
        + jnp.sum(g_contract_all * g_contract_all)
        + jnp.sum(g_head * g_head)
    )
    shared_squares = jnp.sum(g_table * g_table) + jnp.sum(g_norms * g_norms)
    grad_norm = jnp.sqrt(lax.psum(split_squares + first_rank * shared_squares, ("dp", "tensor")))
    factor = clip_limit / jnp.maximum(grad_norm, clip_limit)
    params = (attend_in, attend_out, expand, contract, embed_table, logit_table, norm_params)
    moments_one = (
        attend_in_one,
        attend_out_one,
        expand_one,
        contract_one,
        embed_one,
        logit_one,
        norm_one,
    )
    moments_two = (
        attend_in_two,
        attend_out_two,
        expand_two,
        contract_two,
        embed_two,
        logit_two,
        norm_two,
    )
    results = []
    for index in range(7):
        rate_here = vector_rate if index == 6 else embed_rate if index == 4 else matrix_rate
        decay_here = 0.0 if index == 6 else weight_decay
        results.extend(
            adam_step(
                params[index],
                moments_one[index],
                moments_two[index],
                gradients[index],
                factor,
                rate_here,
                decay_here,
            )
        )
    return (
        results[0],
        results[1],
        results[2],
        results[3],
        results[4],
        results[5],
        results[6],
        results[7],
        results[8],
        results[9],
        results[10],
        results[11],
        results[12],
        results[13],
        results[14],
        results[15],
        results[16],
        results[17],
        results[18],
        results[19],
        results[20],
        loss_sum,
        token_count,
        grad_norm,
    )


def solution(mesh):
    return jax.shard_map(
        body,
        mesh=mesh,
        in_specs=(
            P("dp", None),
            P("dp"),
            P("dp", None),
            P(None, "dp", None, "tensor"),
            P(None, "dp", None, "tensor"),
            P(None, "dp", None, "tensor"),
            P(None, "tensor", "dp"),
            P(None, "tensor", "dp"),
            P(None, "tensor", "dp"),
            P(None, "dp", "tensor"),
            P(None, "dp", "tensor"),
            P(None, "dp", "tensor"),
            P(None, "tensor", "dp"),
            P(None, "tensor", "dp"),
            P(None, "tensor", "dp"),
            P("dp", None),
            P("dp", None),
            P("dp", None),
            P("dp", "tensor"),
            P("dp", "tensor"),
            P("dp", "tensor"),
            P(None, None, "dp"),
            P(None, None, "dp"),
            P(None, None, "dp"),
        ),
        out_specs=(
            P(None, "dp", None, "tensor"),
            P(None, "dp", None, "tensor"),
            P(None, "dp", None, "tensor"),
            P(None, "tensor", "dp"),
            P(None, "tensor", "dp"),
            P(None, "tensor", "dp"),
            P(None, "dp", "tensor"),
            P(None, "dp", "tensor"),
            P(None, "dp", "tensor"),
            P(None, "tensor", "dp"),
            P(None, "tensor", "dp"),
            P(None, "tensor", "dp"),
            P("dp", None),
            P("dp", None),
            P("dp", None),
            P("dp", "tensor"),
            P("dp", "tensor"),
            P("dp", "tensor"),
            P(None, None, "dp"),
            P(None, None, "dp"),
            P(None, None, "dp"),
            P(),
            P(),
            P(),
        ),
        check_vma=False,
    )
```

profile of v0, /device:TPU:0, one launch (start us, length us, event | category | flops | bytes accessed | tf_op | source)
XLA Modules:
  0.0 1645.9 jit_solution(6297815613377147526)
XLA Ops:
  15.6 33.9 %all_gather.22 = bf16[5,2,768]{0,1,2:T(2,128)(2,1)S(1)} all-gather(bf16[5,2,96]{0,1,2:T(2,128)(2,1)S(1)} %copy.215), channel_id=1, replica_groups=mesh['dp'=8,'tensor'=4] {'dp'}, dimensions={2}, use_global_device_ids=true | all-gather | bytes 17280 | tf_op jit(solution)/shard_map/all_gather | solution.py:200
  49.8 33.6 %all_gather.24 = bf16[2,192,768]{1,0,2:T(2,128)(2,1)S(1)} all-gather(bf16[2,192,96]{1,0,2:T(2,128)(2,1)S(1)} %copy.224), channel_id=1, replica_groups=mesh['dp'=8,'tensor'=4] {'dp'}, dimensions={2}, use_global_device_ids=true | all-gather | bytes 663552 | tf_op jit(solution)/shard_map/all_gather | solution.py:195
  88.6 27.2 %slice_reduce_fusion.1 = (f32[768]{0:T(1024)}, f32[768]{0:T(1024)}, f32[768]{0:T(1024)}, f32[768]{0:T(1024)S(1)}, f32[768]{0:T(1024)}, /*index=5*/f32[768]{0:T(1...) fusion(f32[5,2,768]{0,1,2:T(2,128)S(1)} %convert_element_type.203), kind=kLoop, calls=%fused_computation.225 | loop fusion | bytes 61440 | tf_op jit(solution)/shard_map/slice | solution.py:226
  115.8 7.8 fusion.140
  123.7 4.4 copy.272
  128.1 16.1 all-gather.5.cloned.1.call-done
  144.2 8.4 gather_fusion.1
  152.6 4.9 gather_fusion
  162.4 3.1 convolution_convert_fusion.10
  165.5 5.1 reshape.438
  187.7 40.2 %all-reduce.16.cloned.1.call-done = bf16[1028,768]{1,0:T(8,128)(2,1)} async-done(((bf16[1028,768]{1,0:T(8,128)(2,1)}), bf16[1028,768]{1,0:T(8,128)(2,1)}) %all-reduce.16.cloned.1.call-update) | async-done | bytes 1579024 | tf_op jit(solution)/shard_map/psum | solution.py:58
  227.9 3.1 fusion.137
  231.5 51.1 %all-gather.9.cloned.1.call-done = bf16[2,768,768]{2,1,0:T(8,128)(2,1)} async-done(((bf16[2,96,768]{2,1,0:T(8,128)(2,1)}), bf16[2,768,768]{2,1,0:T(8,128)(2,1)}) %all-gather.9.cloned.1.call-update) | async-done | bytes 2359312 | tf_op jit(solution)/shard_map/all_gather | solution.py:196
  282.6 10.8 multiply_convert_fusion.3
  293.4 42.5 %all-gather.11.cloned.1.call-done = bf16[2,768,768]{1,2,0:T(8,128)(2,1)} async-done(((bf16[2,768,96]{1,2,0:T(8,128)(2,1)}), bf16[2,768,768]{1,2,0:T(8,128)(2,1)}) %all-gather.11.cloned.1.call-update) | async-done | bytes 2359312 | tf_op jit(solution)/shard_map/all_gather | solution.py:197
  335.9 4.3 convolution_convert_fusion.7
  340.3 3.2 copy.281
  343.5 6.4 copy.277
  349.9 32.3 %all-reduce.18.cloned.1.call-done = bf16[1028,768]{1,0:T(8,128)(2,1)} async-done(((bf16[1028,768]{1,0:T(8,128)(2,1)}), bf16[1028,768]{1,0:T(8,128)(2,1)}) %all-reduce.18.cloned.1.call-update) | async-done | bytes 1579024 | tf_op jit(solution)/shard_map/psum | solution.py:58
  385.8 2.8 convolution_convert_fusion.9
  388.7 5.1 reshape.439
  409.9 2.8 convolution_convert_fusion.6
  412.8 43.4 %all-reduce.20.cloned.1.call-done = bf16[1028,768]{1,0:T(8,128)(2,1)} async-done(((bf16[1028,768]{1,0:T(8,128)(2,1)}), bf16[1028,768]{1,0:T(8,128)(2,1)}) %all-reduce.20.cloned.1.call-update) | async-done | bytes 1579024 | tf_op jit(solution)/shard_map/psum | solution.py:58
  460.8 9.6 multiply_convert_fusion.2
  478.5 33.3 %all_gather.27 = bf16[768,256]{1,0:T(8,128)(2,1)} all-gather(bf16[96,256]{1,0:T(8,128)(2,1)} %convert_element_type.231), channel_id=1, replica_groups=mesh['dp'=8,'tensor'=4] {'dp'}, dimensions={0}, use_global_device_ids=true | all-gather | bytes 442368 | tf_op jit(solution)/shard_map/all_gather | solution.py:199
  511.9 5.8 all-reduce.22.cloned.1.call-done
  522.9 6.4 pmax.7
  533.2 11.4 all-reduce.4
  546.5 22.1 %all-reduce.3 = (f32[]{:T(128)}, f32[]{:T(128)}) all-reduce(f32[]{:T(128)} %get-tuple-element.224, f32[]{:T(128)} %get-tuple-element.200), channel_id=1, replica_groups=mesh['dp'=8,'tensor'=4] {'dp'}, use_global_device_ids=true, to_apply=%region_23.24 | all-reduce | flops 2 | bytes 16 | tf_op jit(solution)/shard_map/psum | solution.py:240
  570.6 3.4 convolution_convert_fusion.4
  574.1 40.9 %all-reduce.24.cloned.1.call-done = bf16[1028,768]{1,0:T(8,128)(2,1)} async-done(((bf16[1028,768]{1,0:T(8,128)(2,1)}), bf16[1028,768]{1,0:T(8,128)(2,1)}) %all-reduce.24.cloned.1.call-update) | async-done | bytes 1579024 | tf_op jit(solution)/shard_map/psum | solution.py:62
  615.0 4.4 fusion.24
  623.2 4.2 add_convert_fusion.1
  631.2 43.4 %all-reduce.26.cloned.1.call-done = bf16[1028,768]{1,0:T(8,128)(2,1)} async-done(((bf16[1028,768]{1,0:T(8,128)(2,1)}), bf16[1028,768]{1,0:T(8,128)(2,1)}) %all-reduce.26.cloned.1.call-update) | async-done | bytes 1579024 | tf_op jit(solution)/shard_map/psum | solution.py:62
  685.4 5.0 convolution_bitcast_fusion.5
  700.1 4.4 convolution_convert_fusion.2
  705.0 42.9 %all-reduce.28.cloned.1.call-done = bf16[1028,768]{1,0:T(8,128)(2,1)} async-done(((bf16[1028,768]{1,0:T(8,128)(2,1)}), bf16[1028,768]{1,0:T(8,128)(2,1)}) %all-reduce.28.cloned.1.call-update) | async-done | bytes 1579024 | tf_op jit(solution)/shard_map/psum | solution.py:62
  763.3 43.4 %all-reduce.30.cloned.1.call-done = bf16[1028,768]{1,0:T(8,128)(2,1)} async-done(((bf16[1028,768]{1,0:T(8,128)(2,1)}), bf16[1028,768]{1,0:T(8,128)(2,1)}) %all-reduce.30.cloned.1.call-update) | async-done | bytes 1579024 | tf_op jit(solution)/shard_map/psum | solution.py:62
  818.3 4.4 convolution_bitcast_fusion.4
  822.7 7.5 multiply_reduce_fusion
  830.3 4.7 multiply_convert_fusion
  839.9 4.0 convert_element_type.256
  844.0 4.2 convolution_convert_fusion
  848.6 3.8 fusion.117
  852.5 3.9 convolution_bitcast_fusion.6
  858.0 33.7 %all-reduce.32.cloned.1.call-done = bf16[1028,768]{1,0:T(8,128)(2,1)} async-done(((bf16[1028,768]{1,0:T(8,128)(2,1)}), bf16[1028,768]{1,0:T(8,128)(2,1)}) %all-reduce.32.cloned.1.call-update) | async-done | bytes 1579024 | tf_op jit(solution)/shard_map/psum | solution.py:62
  891.7 3.6 fusion.17
  904.9 3.5 copy.264
  908.4 3.2 reshape.433
  912.2 4.4 convolution_bitcast_fusion
  920.9 8.2 copy.246
  929.8 4.0 fusion.48
  937.9 6.8 copy.262
  944.7 8.0 reshape.431
  953.5 4.7 convolution_bitcast_fusion.2
  964.8 4.3 add_add_fusion.5
  969.1 27.4 %scatter_custom_fusion = f32[2304,768]{1,0:T(8,128)} fusion(s32[2056]{0:T(1024)S(1)} %pad_add_fusion, f32[1028,768]{1,0:T(8,128)} %add_add_fusion.5, f32[]{:T(128)} %constant.65.clone.1, f32[]{:T(128)} %constant.61.clone.1), kind=kCustom, calls=%fused_computation.11 | custom fusion | flops 3158016 | bytes 10235912 | tf_op jit(solution)/shard_map/scatter-add | solution.py:275
  1000.9 21.5 %reduce-scatter.23.cloned.1.call-done = f32[96,10]{1,0:T(8,128)} async-done(((f32[768,10]{1,0:T(8,128)}), f32[96,10]{1,0:T(8,128)}) %reduce-scatter.23.cloned.1.call-update) | async-done | bytes 3856
  1024.0 65.0 %reduce-scatter.21.cloned.1.call-done = f32[96,384]{1,0:T(8,128)} async-done(((f32[768,384]{1,0:T(8,128)}), f32[96,384]{1,0:T(8,128)}) %reduce-scatter.21.cloned.1.call-update) | async-done | bytes 147472
  1090.9 170.7 %all-reduce.34.cloned.1.call-done = f32[2,768,768]{1,0,2:T(2,128)} async-done(((f32[2,768,768]{1,0,2:T(2,128)}), f32[2,768,768]{1,0,2:T(2,128)}) %all-reduce.34.cloned.1.call-update) | async-done | bytes 4718608
  1263.9 79.8 %reduce-scatter.19.cloned.1.call-done = f32[96,1152]{1,0:T(8,128)} async-done(((f32[768,1152]{1,0:T(8,128)}), f32[96,1152]{1,0:T(8,128)}) %reduce-scatter.19.cloned.1.call-update) | async-done | bytes 442384
  1347.6 95.2 %reduce-scatter.13.cloned.1.call-done = f32[2,96,768]{2,1,0:T(8,128)} async-done(((f32[2,768,768]{2,1,0:T(8,128)}), f32[2,96,768]{2,1,0:T(8,128)}) %reduce-scatter.13.cloned.1.call-update) | async-done | bytes 589840 | tf_op jit(solution)/shard_map/reduce_scatter | solution.py:287
  1446.6 129.0 %reduce-scatter.17.cloned.1.call-done = f32[288,768]{1,0:T(8,128)} async-done(((f32[2304,768]{1,0:T(8,128)}), f32[288,768]{1,0:T(8,128)}) %reduce-scatter.17.cloned.1.call-update) | async-done | bytes 884752 | tf_op jit(solution)/shard_map/reduce_scatter | solution.py:289
  1580.1 39.4 %psum.109 = f32[]{:T(128)} all-reduce(f32[]{:T(128)S(6)} %add.412), channel_id=1, replica_groups=mesh['dp'=8,'tensor'=4] {'dp','tensor'}, use_global_device_ids=true, to_apply=%region_66.67 | all-reduce | flops 1 | bytes 8 | tf_op jit(solution)/shard_map/psum | solution.py:303
  (549 shorter events, 204.4 us)
Async XLA Ops:
  7.2 8.3 copy-start.69
  7.2 108.6 %all-gather.7.cloned.1.call-start = ((), (), s32[]{:S(2)}) async-start(), calls=%async_computation.7 | async-start | bytes 2654208 | tf_op jit(solution)/shard_map/all_gather | solution.py:194
  9.5 134.7 %all-gather.5.cloned.1.call-start = ((), (), s32[]{:S(2)}) async-start(), calls=%async_computation.6 | async-start | bytes 3981312 | tf_op jit(solution)/shard_map/all_gather | solution.py:198
  11.6 216.3 %all-reduce.16.cloned.1.call-start = ((), (), s32[]{:S(2)}) async-start(), calls=%async_computation.8 | async-start | bytes 3170304 | tf_op jit(solution)/shard_map/psum | solution.py:58
  115.8 46.0 %copy-start.104 = (f32[768]{0:T(1024)}, f32[768]{0:T(1024)S(1)}, u32[]{:S(2)}) copy-start(f32[768]{0:T(1024)S(1)} %get-tuple-element.170) | copy-start | bytes 9220
  115.8 166.8 %copy-start.106 = (f32[768]{0:T(1024)}, f32[768]{0:T(1024)S(1)}, u32[]{:S(2)}) copy-start(f32[768]{0:T(1024)S(1)} %get-tuple-element.168) | copy-start | bytes 9220
  115.8 268.8 %copy-start.112 = (f32[768]{0:T(1024)}, f32[768]{0:T(1024)S(1)}, u32[]{:S(2)}) copy-start(f32[768]{0:T(1024)S(1)} %get-tuple-element.166) | copy-start | bytes 9220
  115.8 343.3 %copy-start.109 = (f32[768]{0:T(1024)}, f32[768]{0:T(1024)S(1)}, u32[]{:S(2)}) copy-start(f32[768]{0:T(1024)S(1)} %get-tuple-element.164) | copy-start | bytes 9220
  144.2 8.4 copy-start.2
  185.9 96.7 %all-gather.9.cloned.1.call-start = ((), (), s32[]{:S(2)}) async-start(), calls=%async_computation.9 | async-start | bytes 2654208 | tf_op jit(solution)/shard_map/all_gather | solution.py:196
  186.8 149.1 %all-gather.11.cloned.1.call-start = ((), (), s32[]{:S(2)}) async-start(), calls=%async_computation.10 | async-start | bytes 2654208 | tf_op jit(solution)/shard_map/all_gather | solution.py:197
  187.6 194.6 %all-reduce.18.cloned.1.call-start = ((), (), s32[]{:S(2)}) async-start(), calls=%async_computation.11 | async-start | bytes 3170304 | tf_op jit(solution)/shard_map/psum | solution.py:58
  230.9 151.3 %copy-start.3 = (f32[1028,768]{1,0:T(8,128)}, f32[1028,768]{1,0:T(8,128)S(1)}, u32[]{:S(2)}) copy-start(f32[1028,768]{1,0:T(8,128)S(1)} %get-tuple-element.213) | copy-start | bytes 9474052
  230.9 51.7 %copy-start.140 = (f32[768]{0:T(1024)S(1)}, f32[768]{0:T(1024)}, u32[]{:S(2)}) copy-start(f32[768]{0:T(1024)} %get-tuple-element.167) | copy-start | bytes 9220
  231.5 61.9 %copy-start.93 = (f32[1028]{0:T(1024)}, f32[1028]{0:T(1024)S(1)}, u32[]{:S(2)}) copy-start(f32[1028]{0:T(1024)S(1)} %multiply_reduce_fusion.7) | copy-start | bytes 12340
  231.5 61.9 %copy-start.87 = (f32[1028]{0:T(1024)}, f32[1028]{0:T(1024)S(1)}, u32[]{:S(2)}) copy-start(f32[1028]{0:T(1024)S(1)} %fusion.106) | copy-start | bytes 12340
  340.2 115.9 %all-reduce.20.cloned.1.call-start = ((), (), s32[]{:S(2)}) async-start(), calls=%async_computation.12 | async-start | bytes 3170304 | tf_op jit(solution)/shard_map/psum | solution.py:58
  406.3 49.9 %copy-start.6 = (f32[1028,768]{1,0:T(8,128)S(1)}, f32[1028,768]{1,0:T(8,128)}, u32[]{:S(2)}) copy-start(f32[1028,768]{1,0:T(8,128)} %copy-done.5) | copy-start | bytes 9474052
  412.7 105.0 %all-reduce.22.cloned.1.call-start = ((), (), s32[]{:S(2)}) async-start(), calls=%async_computation.13 | async-start | bytes 3170304 | tf_op jit(solution)/shard_map/psum | solution.py:58
  458.0 12.5 copy-start.8
  459.1 11.3 copy-start.101
  460.8 10.8 copy-start.151
  471.6 46.1 %copy-start.9 = (f32[1028,768]{1,0:T(8,128)S(1)}, f32[1028,768]{1,0:T(8,128)}, u32[]{:S(2)}) copy-start(f32[1028,768]{1,0:T(8,128)} %copy-done.8) | copy-start | bytes 9474052
  474.3 140.7 %all-reduce.24.cloned.1.call-start = ((), (), s32[]{:S(2)}) async-start(), calls=%async_computation.14 | async-start | bytes 3170304 | tf_op jit(solution)/shard_map/psum | solution.py:62
  533.2 81.8 %copy-start.81 = (f32[1028]{0:T(1024)S(1)}, f32[1028]{0:T(1024)}, u32[]{:S(2)}) copy-start(f32[1028]{0:T(1024)} %copy-done.80) | copy-start | bytes 12340
  574.0 100.6 %all-reduce.26.cloned.1.call-start = ((), (), s32[]{:S(2)}) async-start(), calls=%async_computation.15 | async-start | bytes 3170304 | tf_op jit(solution)/shard_map/psum | solution.py:62
  620.6 6.7 copy-start.31
  620.7 6.7 copy-start.124
  631.2 45.8 %copy-start.98 = (f32[1028]{0:T(1024)S(1)}, f32[1028]{0:T(1024)}, u32[]{:S(2)}) copy-start(f32[1028]{0:T(1024)} %copy-done.97) | copy-start | bytes 12340
  631.2 45.8 %copy-start.102 = (f32[1028]{0:T(1024)S(1)}, f32[1028]{0:T(1024)}, u32[]{:S(2)}) copy-start(f32[1028]{0:T(1024)} %copy-done.101) | copy-start | bytes 12340
  631.2 116.8 %all-reduce.28.cloned.1.call-start = ((), (), s32[]{:S(2)}) async-start(), calls=%async_computation.16 | async-start | bytes 3170304 | tf_op jit(solution)/shard_map/psum | solution.py:62
  682.3 8.1 slice-start.2
  700.1 47.8 %copy-start.7 = (f32[1028,768]{1,0:T(8,128)S(1)}, f32[1028,768]{1,0:T(8,128)}, u32[]{:S(2)}) copy-start(f32[1028,768]{1,0:T(8,128)} %copy-done.5) | copy-start | bytes 9474052
  700.1 47.8 %copy-start.113 = (f32[768]{0:T(1024)S(1)}, f32[768]{0:T(1024)}, u32[]{:S(2)}) copy-start(f32[768]{0:T(1024)} %copy-done.112) | copy-start | bytes 9220
  704.5 45.8 %copy-start.96 = (f32[1028]{0:T(1024)S(1)}, f32[1028]{0:T(1024)}, u32[]{:S(2)}) copy-start(f32[1028]{0:T(1024)} %copy-done.95) | copy-start | bytes 12340
  704.5 45.8 %copy-start.90 = (f32[1028]{0:T(1024)S(1)}, f32[1028]{0:T(1024)}, u32[]{:S(2)}) copy-start(f32[1028]{0:T(1024)} %copy-done.89) | copy-start | bytes 12340
  704.5 102.1 %all-reduce.30.cloned.1.call-start = ((), (), s32[]{:S(2)}) async-start(), calls=%async_computation.17 | async-start | bytes 3170304 | tf_op jit(solution)/shard_map/psum | solution.py:62
  760.6 46.1 %copy-start.4 = (f32[1028,768]{1,0:T(8,128)S(1)}, f32[1028,768]{1,0:T(8,128)}, u32[]{:S(2)}) copy-start(f32[1028,768]{1,0:T(8,128)} %copy-done.3) | copy-start | bytes 9474052
  760.6 46.1 %copy-start.107 = (f32[768]{0:T(1024)S(1)}, f32[768]{0:T(1024)}, u32[]{:S(2)}) copy-start(f32[768]{0:T(1024)} %copy-done.106) | copy-start | bytes 9220
  763.2 45.8 %copy-start.94 = (f32[1028]{0:T(1024)S(1)}, f32[1028]{0:T(1024)}, u32[]{:S(2)}) copy-start(f32[1028]{0:T(1024)} %copy-done.93) | copy-start | bytes 12340
  763.2 45.8 %copy-start.88 = (f32[1028]{0:T(1024)S(1)}, f32[1028]{0:T(1024)}, u32[]{:S(2)}) copy-start(f32[1028]{0:T(1024)} %copy-done.87) | copy-start | bytes 12340
  763.2 128.4 %all-reduce.32.cloned.1.call-start = ((), (), s32[]{:S(2)}) async-start(), calls=%async_computation.20 | async-start | bytes 3170304 | tf_op jit(solution)/shard_map/psum | solution.py:62
  818.3 11.9 slice-start
  822.7 7.5 slice-start.1
  848.3 151.1 %reduce-scatter.15.cloned.1.call-start = ((), (), s32[]{:S(2)}) async-start(), calls=%async_computation.19 | async-start | bytes 884736 | tf_op jit(solution)/shard_map/reduce_scatter | solution.py:290
  852.3 170.0 %reduce-scatter.23.cloned.1.call-start = ((), (), s32[]{:S(2)}) async-start(), calls=%async_computation.24 | async-start | bytes 442368
  856.3 35.3 %copy-start.79 = (f32[1028]{0:T(1024)S(1)}, f32[1028]{0:T(1024)}, u32[]{:S(2)}) copy-start(f32[1028]{0:T(1024)} %copy-done.78) | copy-start | bytes 12340
  856.3 35.3 %copy-start.105 = (f32[768]{0:T(1024)S(1)}, f32[768]{0:T(1024)}, u32[]{:S(2)}) copy-start(f32[768]{0:T(1024)} %copy-done.104) | copy-start | bytes 9220
  857.9 37.3 %copy-start.92 = (f32[1028]{0:T(1024)S(1)}, f32[1028]{0:T(1024)}, u32[]{:S(2)}) copy-start(f32[1028]{0:T(1024)} %copy-done.91) | copy-start | bytes 12340
  857.9 37.3 %copy-start.86 = (f32[1028]{0:T(1024)S(1)}, f32[1028]{0:T(1024)}, u32[]{:S(2)}) copy-start(f32[1028]{0:T(1024)} %copy-done.85) | copy-start | bytes 12340
  902.5 186.5 %reduce-scatter.21.cloned.1.call-start = ((), (), s32[]{:S(2)}) async-start(), calls=%async_computation.23 | async-start | bytes 1327104
  904.9 7.2 copy-start.126
  911.7 349.9 %all-reduce.34.cloned.1.call-start = ((), (), s32[]{:S(2)}) async-start(), calls=%async_computation.25 | async-start | bytes 9437184
  929.1 414.6 %reduce-scatter.19.cloned.1.call-start = ((), (), s32[]{:S(2)}) async-start(), calls=%async_computation.22 | async-start | bytes 3981312
  952.8 490.0 %reduce-scatter.13.cloned.1.call-start = ((), (), s32[]{:S(2)}) async-start(), calls=%async_computation.18 | async-start | bytes 5308416 | tf_op jit(solution)/shard_map/reduce_scatter | solution.py:287
  962.9 612.6 %reduce-scatter.17.cloned.1.call-start = ((), (), s32[]{:S(2)}) async-start(), calls=%async_computation.21 | async-start | bytes 7962624 | tf_op jit(solution)/shard_map/reduce_scatter | solution.py:289
  1620.2 8.1 copy-start.127
  1620.3 9.6 copy-start.70
  1621.8 10.1 copy-start.59
  1621.8 10.1 copy-start.71
  1621.8 10.1 copy-start.72
  1626.2 7.2 copy-start.76
  1626.2 7.2 copy-start.77
  1628.4 5.8 copy-start.61
  (123 other events, 358.4 us)
Sparse Core Ops, SparseCore 0:
  10.8 66.5 all-gather.6
  80.1 64.0 all-gather.4
  186.1 41.7 all-reduce.15
  230.5 52.0 all-gather.8
  285.2 50.6 all-gather.10
  340.3 41.7 all-reduce.17
  412.8 43.2 all-reduce.19
  474.4 43.2 all-reduce.21
  574.2 40.7 all-reduce.23
  631.3 43.2 all-reduce.25
  704.7 43.2 all-reduce.27
  763.3 43.2 all-reduce.29
  848.3 43.2 all-reduce.31
  895.4 62.4 reduce-scatter.14
  961.9 60.4 reduce-scatter.22
  1026.0 63.0 reduce-scatter.20
  1092.9 168.6 all-reduce.33
  1265.5 78.1 reduce-scatter.18
  1347.8 94.9 reduce-scatter.12
  1446.8 128.7 reduce-scatter.16
where the time goes:
time: 1650 us
  waiting for transfers between devices  997 us (60%)
  local copies, waits for them, and re-layouts  188 us (11%)
  blocking collectives  180 us (11%)
  other arithmetic  132 us (8%)
  matrix products  122 us (7%)
  between operations  23.6 us (1%)
    unnamed x24, waiting for transfers between devices  337 us
    psum x5, waiting for transfers between devices, input_total(): lax.psum(piece_sum.astype(jnp.bfloat16), 'tensor').astype(jnp.float32)  204 us
    reduce_scatter x1, waiting for transfers between devices, body(): lax.psum_scatter(g_table, 'dp', scatter_dimension=0, tiled=True)  129 us
    psum x4, waiting for transfers between devices, branch_total(): lax.psum(piece_sum.astype(jnp.bfloat16), 'tensor').astype(jnp.float32)  122 us
    reduce_scatter x1, waiting for transfers between devices, body(): lax.psum_scatter(g_expand_all, 'dp', scatter_dimension=1, tiled=True)  95.2 us
    unnamed x365, local copies, waits for them, and re-layouts  94.6 us
    all_gather x1, waiting for transfers between devices, body(): lax.all_gather(expand.astype(jnp.bfloat16), 'dp', axis=1, tiled=True)  51.1 us
    all_gather x1, waiting for transfers between devices, body(): lax.all_gather(contract.astype(jnp.bfloat16), 'dp', axis=2, tiled=True)  42.5 us
  transfers between devices with their start and end apart: 20, of which 18 were waited for; matrix products, arithmetic and copies ran while one was open for 12% of the time, Pallas kernels for 0%

commit v1 on v0

v1 whole, which is shorter than its diff:
```python
import functools

import jax
import jax.numpy as jnp
from jax import lax
from jax.experimental import pallas as pl
from jax.experimental.pallas import tpu as pltpu
from jax.sharding import PartitionSpec as P

HEADS = 16
CODES = 1024
CLASSES = 1000
LAYERS = 2
STEP = 10
SEQ = 257

beta_one = 0.9
beta_two = 0.96
matrix_rate = 0.02
embed_rate = 0.5
vector_rate = 0.25
weight_decay = 0.045
epsilon = 1e-10
clip_limit = 0.02
norm_epsilon = 1e-06
low = jnp.bfloat16
full = jnp.float32


def matmul(left, right):
    return jnp.dot(left, right, preferred_element_type=full)


def matmul_left(left, right):
    return lax.dot_general(left, right, (((0,), (0,)), ((), ())), preferred_element_type=full)


def matmul_right(left, right):
    return lax.dot_general(left, right, (((1,), (1,)), ((), ())), preferred_element_type=full)


def layer_norm(stream, scaling, offset):
    average = jnp.mean(stream, axis=-1, keepdims=True)
    centred = stream - average
    variance = jnp.mean(centred * centred, axis=-1, keepdims=True)
    return centred * lax.rsqrt(variance + norm_epsilon) * scaling + offset


def norm_back(stream, scaling, offset, gradient):
    normed_out, pull = jax.vjp(layer_norm, stream, scaling, offset)
    return pull(gradient)


def gelu_exact(values):
    return jax.nn.gelu(values, approximate=False)


def attend_forward_kernel(images, heads, width, *refs):
    count = len(refs) // 2
    scale = width ** (-0.5)
    for joined, blended in zip(refs[:count], refs[count:]):
        for image in range(images):
            rows = pl.ds(image * SEQ, SEQ)
            for head in range(heads):
                at = head * width
                query = joined[rows, at : at + width]
                key = joined[rows, (heads * width + at) : (heads * width + at + width)]
                value = joined[rows, (2 * heads * width + at) : (2 * heads * width + at + width)]
                scores = matmul_right(query, key) * scale
                top = jnp.max(scores, axis=-1, keepdims=True)
                weights = jnp.exp(scores - top)
                weights = weights / jnp.sum(weights, axis=-1, keepdims=True)
                blended[rows, at : at + width] = matmul(weights.astype(low), value).astype(low)


def attend_forward(joined, images, heads, width):
    rows = joined[0].shape[0]
    return pl.pallas_call(
        functools.partial(attend_forward_kernel, images, heads, width),
        out_shape=[jax.ShapeDtypeStruct((rows, heads * width), low) for _ in joined],
        in_specs=[pl.BlockSpec(memory_space=pltpu.VMEM)] * len(joined),
        out_specs=[pl.BlockSpec(memory_space=pltpu.VMEM)] * len(joined),
        compiler_params=pltpu.CompilerParams(vmem_limit_bytes=32 * 1024 * 1024),
        cost_estimate=pl.CostEstimate(
            flops=len(joined) * images * heads * SEQ * SEQ * width * 4,
            bytes_accessed=len(joined) * rows * heads * width * 8,
            transcendentals=len(joined) * images * heads * SEQ * SEQ,
        ),
    )(*joined)


def attend_backward_kernel(images, heads, width, *refs):
    count = len(refs) // 3
    scale = width ** (-0.5)
    for joined, grad, out in zip(refs[:count], refs[count : 2 * count], refs[2 * count :]):
        for image in range(images):
            rows = pl.ds(image * SEQ, SEQ)
            for head in range(heads):
                at = head * width
                spots = [pl.ds(part * heads * width + at, width) for part in range(3)]
                query, key, value = [joined[rows, spot] for spot in spots]
                up = grad[rows, at : at + width]
                scores = matmul_right(query, key) * scale
                top = jnp.max(scores, axis=-1, keepdims=True)
                weights = jnp.exp(scores - top)
                weights = weights / jnp.sum(weights, axis=-1, keepdims=True)
                pulled = matmul_right(up, value)
                total = jnp.sum(weights * pulled, axis=-1, keepdims=True)
                moved = (weights * (pulled - total)).astype(low)
                out[rows, spots[0]] = (matmul(moved, key) * scale).astype(low)
                out[rows, spots[1]] = (matmul_left(moved, query) * scale).astype(low)
                out[rows, spots[2]] = matmul_left(weights.astype(low), up).astype(low)


def attend_backward(joined, grads, images, heads, width):
    return pl.pallas_call(
        functools.partial(attend_backward_kernel, images, heads, width),
        out_shape=[jax.ShapeDtypeStruct(block.shape, low) for block in joined],
        in_specs=[pl.BlockSpec(memory_space=pltpu.VMEM)] * (2 * len(joined)),
        out_specs=[pl.BlockSpec(memory_space=pltpu.VMEM)] * len(joined),
        compiler_params=pltpu.CompilerParams(vmem_limit_bytes=32 * 1024 * 1024),
        cost_estimate=pl.CostEstimate(
            flops=len(joined) * images * heads * SEQ * SEQ * width * 10,
            bytes_accessed=len(joined) * joined[0].shape[0] * heads * width * 14,
            transcendentals=len(joined) * images * heads * SEQ * SEQ,
        ),
    )(*joined, *grads)


MESH = pl.DeviceIdType.MESH


def factors(dp, tensor):
    return [("tensor", tensor // 2, 2), ("tensor", 2, 1), ("dp", dp // 2, 2), ("dp", 2, 1)]


OUTER, PAIR, LONG, NEAR = range(4)
ORDERS = {
    "a": (LONG, NEAR, OUTER, PAIR),
    "b": (LONG, OUTER, NEAR, PAIR),
    "d": (OUTER, LONG, NEAR, PAIR),
    "e": (NEAR, LONG, OUTER, PAIR),
}


def place_of(dims):
    return [(lax.axis_index(axis) // stride) % size for axis, size, stride in dims]


def peer_of(dims, here, dim, move):
    there = list(here)
    there[dim] = lax.rem(here[dim] + move, dims[dim][1])
    found = {"dp": 0, "tensor": 0}
    for (axis, size, stride), at in zip(dims, there):
        found[axis] = found[axis] + at * stride
    return (found["dp"], found["tensor"])


def greet(dims, here):
    barrier = pltpu.get_barrier_semaphore()
    count = 0
    for dim, (axis, size, stride) in enumerate(dims):
        for move in range(1, size):
            pl.semaphore_signal(
                barrier, inc=1, device_id=peer_of(dims, here, dim, move), device_id_type=MESH
            )
            count += 1
    pl.semaphore_wait(barrier, count)


def gather_units(rows):
    tiles = rows // 16
    if rows % 16 or tiles < 4:
        return [[(0, rows, "a")]]
    if tiles == 6:
        cuts = [[("a", 1), ("b", 1), ("d", 1)], [("a", 1), ("b", 1), ("e", 1)]]
    else:
        cuts = [[("a", 1), ("b", 1)], [("a", 1), ("b", 1), ("d", tiles - 4)]]
    units, row = [], 0
    for cut in cuts:
        unit = []
        for order, count in cut:
            unit.append((row, 16 * count, order))
            row += 16 * count
        units.append(unit)
    return units


def gather_kernel(dims, shapes, *refs):
    count = len(shapes)
    pieces, wholes, (send, recv, own) = refs[:count], refs[count : 2 * count], refs[2 * count :]
    here = place_of(dims)
    greet(dims, here)
    copies_own = [
        pltpu.make_async_copy(pieces[at], wholes[at].at[tuple(here)], own.at[at]) for at in range(count)
    ]
    for copy in copies_own:
        copy.start()
    slot, units = 0, []
    for chunk, (rows, width) in enumerate(shapes):
        for unit in gather_units(rows):
            stages = [[], [], [], []]
            for row, size, order in unit:
                span = (pl.ds(row, size),) if size != rows else ()
                for stage, dim in enumerate(ORDERS[order]):
                    done = ORDERS[order][:stage]
                    block = wholes[chunk].at[
                        tuple(slice(None) if at in done else here[at] for at in range(4)) + span
                    ]
                    source = block
                    if stage == 0:
                        source = pieces[chunk].at[span] if span else pieces[chunk]
                    for move in range(1, dims[dim][1]):
                        stages[stage].append(
                            pltpu.make_async_remote_copy(
                                src_ref=source,
                                dst_ref=block,
                                send_sem=send.at[slot],
                                recv_sem=recv.at[slot],
                                device_id=peer_of(dims, here, dim, move),
                                device_id_type=MESH,
                            )
                        )
                        slot += 1
            units.append((chunk, stages))
    ready = set()
    for tick in range(len(units) + 8):
        for at, (chunk, stages) in enumerate(units):
            if (tick - at) % 2 or not 0 <= tick - at <= 8:
                continue
            stage = (tick - at) // 2
            if stage:
                for copy in stages[stage - 1]:
                    copy.wait_recv()
            if stage == 1 and chunk not in ready:
                copies_own[chunk].wait()
                ready.add(chunk)
            if stage < 4:
                for copy in stages[stage]:
                    copy.start()
    for chunk, stages in units:
        for stage in stages:
            for copy in stage:
                copy.wait_send()


def gather_all(dims, pieces):
    shapes = [piece.shape for piece in pieces]
    sizes = [size for axis, size, stride in dims]
    slots = sum(sum(size - 1 for size in sizes) * len(u) for r, w in shapes for u in gather_units(r))
    wholes = pl.pallas_call(
        functools.partial(gather_kernel, dims, shapes),
        out_shape=[jax.ShapeDtypeStruct((*sizes, *shape), low) for shape in shapes],
        in_specs=[pl.BlockSpec(memory_space=pl.ANY)] * len(shapes),
        out_specs=[pl.BlockSpec(memory_space=pl.ANY)] * len(shapes),
        scratch_shapes=[
            pltpu.SemaphoreType.DMA((slots,)),
            pltpu.SemaphoreType.DMA((slots,)),
            pltpu.SemaphoreType.DMA((len(shapes),)),
        ],
        compiler_params=pltpu.CompilerParams(collective_id=0, has_side_effects=True),
    )(*pieces)
    return [whole.reshape(sizes[0] * sizes[1], -1, whole.shape[-1]) for whole in wholes]


def adam_step(weight, moment_one, moment_two, gradient, factor, rate_here, decay_here):
    gradient = gradient * factor
    moment_one = beta_one * moment_one + (1.0 - beta_one) * gradient
    moment_two = beta_two * moment_two + (1.0 - beta_two) * gradient * gradient
    correct_one = 1.0 - beta_one**STEP
    correct_two = 1.0 - beta_two**STEP
    weight = weight - rate_here * (
        moment_one / correct_one / (jnp.sqrt(moment_two / correct_two) + epsilon)
        + decay_here * weight
    )
    return [weight, moment_one, moment_two]


def masks_of(size):
    return [1 << bit for bit in reversed(range(size.bit_length() - 1))]


class Exchange:
    def __init__(self, dp, tensor):
        self.dp, self.tensor = dp, tensor
        self.dp_masks, self.tensor_masks = masks_of(dp), masks_of(tensor)

    def orders(self, kind):
        depth = [("dp", mask) for mask in self.dp_masks]
        outer = [("tensor", mask) for mask in self.tensor_masks]
        if kind == 0:
            return depth + outer
        return depth[:-1] + outer[:-1] + depth[-1:] + outer[-1:]

    def swap(self, value, axis, mask):
        size = self.dp if axis == "dp" else self.tensor
        return lax.ppermute(value, axis, [(at, at ^ mask) for at in range(size)])

    def reduce(self, blocks, kind, last=full):
        width = blocks[0].shape[-1]
        left = [("tensor", mask) for mask in self.tensor_masks] + [("dp", mask) for mask in self.dp_masks]
        value = jnp.stack(blocks).reshape((2,) * len(left) + (-1, width))
        order = self.orders(kind)[::-1]
        for step, (axis, mask) in enumerate(order):
            kind_here = last if step == len(order) - 1 else low
            bit = (lax.axis_index(axis) & mask) // mask
            place = left.index((axis, mask))
            left.remove((axis, mask))
            away = lax.dynamic_index_in_dim(value, 1 - bit, place, keepdims=False)
            kept = lax.dynamic_index_in_dim(value, bit, place, keepdims=False)
            value = kept + self.swap(away.astype(kind_here), axis, mask).astype(full)
        return value

    def spread(self, piece):
        held = piece[None]
        for mask in self.tensor_masks[::-1]:
            upper = (lax.axis_index("tensor") & mask) != 0
            other = self.swap(held, "tensor", mask)
            held = jnp.where(
                upper, jnp.concatenate([other, held], 0), jnp.concatenate([held, other], 0)
            )
        return held


def body(
    dp,
    tensor,
    image_codes,
    labels,
    mask_flags,
    attend_in,
    attend_in_one,
    attend_in_two,
    attend_out,
    attend_out_one,
    attend_out_two,
    expand,
    expand_one,
    expand_two,
    contract,
    contract_one,
    contract_two,
    embed_table,
    embed_one,
    embed_two,
    logit_table,
    logit_one,
    logit_two,
    norm_params,
    norm_one,
    norm_two,
):
    links = Exchange(dp, tensor)
    own = lax.axis_index("tensor")
    depth = attend_in.shape[1]
    model = depth * dp
    part = attend_in.shape[3]
    norms = norm_params.shape[0]

    share = embed_table.shape[0] // tensor
    embed_own = lax.dynamic_slice_in_dim(embed_table, own * share, share, 0).astype(low)
    norm_flat = norm_params.astype(low).reshape(-1)
    norm_rows = -(-norm_flat.shape[0] // model)
    norm_flat = jnp.pad(norm_flat, (0, norm_rows * model - norm_flat.shape[0])).reshape(norm_rows, model)
    lines = -(-(share + norm_rows) // 16) * 16
    embed_piece = jnp.concatenate(
        [embed_own, norm_flat, jnp.zeros((lines - share - norm_rows, model), low)], 0
    )
    attend_pieces, expand_pieces, contract_pieces = [], [], []
    for layer in range(LAYERS):
        planes = attend_in[layer].astype(low)
        attend_pieces.append(
            jnp.concatenate([planes[:, 0], planes[:, 1], planes[:, 2], attend_out[layer].astype(low).T], 1)
        )
        expand_pieces.append(expand[layer].astype(low))
        contract_pieces.append(contract[layer].astype(low).T)

    pieces = [embed_piece]
    for layer in range(LAYERS):
        pieces += [attend_pieces[layer], expand_pieces[layer], contract_pieces[layer]]
    gathered = gather_all(factors(dp, tensor), pieces + [logit_table.astype(low)])
    table_all, w_head = gathered[0], gathered[-1]
    w_attend, w_expand, w_contract = gathered[1:-1:3], gathered[2:-1:3], gathered[3:-1:3]
    spots = list(range(tensor))

    gains = table_all[0].reshape(dp, lines, model)[:, share : share + norm_rows].reshape(dp, -1)
    gains = gains[:, : norms * 2 * depth].reshape(dp, norms, 2, depth).transpose(1, 2, 0, 3)
    gains = gains.reshape(norms, 2, model).astype(full)
    table = jnp.concatenate(
        [
            table_all[at].reshape(dp, lines, model)[:, :share].reshape(-1, model)
            for at in spots
        ],
        0,
    )

    token_count = lax.psum(jnp.sum(mask_flags.astype(full)), "dp")
    images = labels.shape[0] // tensor
    codes_own = lax.dynamic_slice_in_dim(image_codes, own * images, images, 0)
    flags_own = lax.dynamic_slice_in_dim(mask_flags, own * images, images, 0)
    labels_own = lax.dynamic_slice_in_dim(labels, own * images, images, 0)
    code_rows = jnp.where(flags_own == 1, CODES, codes_own)
    row_index = jnp.concatenate([(CODES + 1 + labels_own)[:, None], code_rows], axis=1).reshape(-1)
    place_rows = jnp.tile(CODES + 1 + CLASSES + jnp.arange(SEQ, dtype=jnp.int32), images)
    targets = jnp.concatenate([jnp.zeros((images, 1), jnp.int32), codes_own], axis=1).reshape(-1)
    weights_loss = jnp.concatenate(
        [jnp.zeros((images, 1), full), flags_own.astype(full)], axis=1
    ).reshape(-1)

    def spot_of(rows):
        block, inside = rows // (share * tensor), rows % (share * tensor)
        return (inside // share) * (share * dp) + block * share + inside % share

    row_numbers = jnp.arange(table.shape[0], dtype=jnp.int32)[:, None]
    picks = (
        (row_numbers == spot_of(row_index)[None, :]).astype(full)
        + (row_numbers == spot_of(place_rows)[None, :]).astype(full)
    ).astype(low)

    head_count = HEADS // tensor
    head_width = model // HEADS
    stream = matmul_left(picks, table)
    saved_all = []
    for layer in range(LAYERS):
        gain, gain_two = gains[2 * layer], gains[2 * layer + 1]
        normed = layer_norm(stream, gain[0], gain[1]).astype(low)
        joined = [matmul(normed, w_attend[layer][at][:, : 3 * part]).astype(low) for at in spots]
        blended = attend_forward(joined, images, head_count, head_width)
        middle = stream + sum(
            matmul_right(blended[at], w_attend[layer][at][:, 3 * part :]) for at in spots
        )
        normed_two = layer_norm(middle, gain_two[0], gain_two[1]).astype(low)
        hidden = [matmul(normed_two, w_expand[layer][at]) for at in spots]
        active = [gelu_exact(block).astype(low) for block in hidden]
        result = middle + sum(matmul_right(active[at], w_contract[layer][at]) for at in spots)
        saved_all.append((stream, normed, joined, blended, middle, normed_two, hidden, active))
        stream = result

    final_gain = gains[2 * LAYERS]
    final = layer_norm(stream, final_gain[0], final_gain[1]).astype(low)
    logits = jnp.concatenate([matmul(final, w_head[at]) for at in spots], 1)
    local = logit_table.shape[1]
    code_ids = jnp.arange(local * tensor, dtype=jnp.int32)
    is_target = (targets[:, None] == code_ids[None, :]).astype(full)
    peak = jnp.max(logits, axis=1, keepdims=True)
    log_total = peak + jnp.log(jnp.sum(jnp.exp(logits - peak), axis=1, keepdims=True))
    picked = jnp.sum(is_target * logits, axis=1)
    loss_sum = lax.psum(jnp.sum((log_total[:, 0] - picked) * weights_loss), ("dp", "tensor"))
    grad_logits = (
        (jnp.exp(logits - log_total) - is_target) * (weights_loss / token_count)[:, None]
    ).astype(low)
    grad_logits = [grad_logits[:, at * local : (at + 1) * local] for at in spots]
    g_head = links.reduce([matmul_left(final, grad_logits[at]) for at in spots], 0)
    grad_final = sum(matmul_right(grad_logits[at], w_head[at]) for at in spots)
    gradient, final_scale, final_offset = norm_back(stream, final_gain[0], final_gain[1], grad_final)

    norm_grads = [None] * norms
    norm_grads[2 * LAYERS] = jnp.stack([final_scale, final_offset])
    g_attend, g_expand, g_contract = [None] * LAYERS, [None] * LAYERS, [None] * LAYERS
    for layer in reversed(range(LAYERS)):
        stream, normed, joined, blended, middle, normed_two, hidden, active = saved_all[layer]
        gain, gain_two = gains[2 * layer], gains[2 * layer + 1]
        grad_low = gradient.astype(low)
        g_contract[layer] = links.reduce([matmul_left(grad_low, active[at]) for at in spots], 1)
        grad_hidden = []
        for at in spots:
            grad_active = matmul(grad_low, w_contract[layer][at])
            gelu_out, gelu_pull = jax.vjp(gelu_exact, hidden[at])
            grad_hidden.append(gelu_pull(grad_active)[0].astype(low))
        g_expand[layer] = links.reduce([matmul_left(normed_two, grad_hidden[at]) for at in spots], 0)
        grad_normed = sum(matmul_right(grad_hidden[at], w_expand[layer][at]) for at in spots)
        grad_mid, scale_two, offset_two = norm_back(middle, gain_two[0], gain_two[1], grad_normed)
        gradient = gradient + grad_mid
        grad_low = gradient.astype(low)
        grad_blended = [matmul(grad_low, w_attend[layer][at][:, 3 * part :]).astype(low) for at in spots]
        grad_joined = attend_backward(joined, grad_blended, images, head_count, head_width)
        g_attend[layer] = links.reduce(
            [
                jnp.concatenate(
                    [matmul_left(normed, grad_joined[at]), matmul_left(grad_low, blended[at])], 1
                )
                for at in spots
            ],
            1,
        )
        grad_normed = sum(
            matmul_right(grad_joined[at], w_attend[layer][at][:, : 3 * part]) for at in spots
        )
        grad_first, scale_one, offset_one = norm_back(stream, gain[0], gain[1], grad_normed)
        gradient = gradient + grad_first
        norm_grads[2 * layer] = jnp.stack([scale_one, offset_one])
        norm_grads[2 * layer + 1] = jnp.stack([scale_two, offset_two])

    upper = gradient.astype(low)
    lower = (gradient - upper.astype(full)).astype(low)
    g_table = matmul(jnp.concatenate([picks, picks], 1), jnp.concatenate([upper, lower], 0))
    g_table = g_table.reshape(tensor, dp, share, model)
    g_norms = jnp.stack(norm_grads).reshape(norms, 2, dp, depth).transpose(2, 0, 1, 3).reshape(dp, -1)
    norm_size = g_norms.shape[1]
    norm_share = -(-norm_size // tensor)
    g_norms = jnp.pad(g_norms, ((0, 0), (0, norm_share * tensor - norm_size))).reshape(dp, tensor, norm_share)
    norm_lines = -(-norm_share // model)
    g_norms = jnp.pad(g_norms, ((0, 0), (0, 0), (0, norm_lines * model - norm_share)))
    g_norms = g_norms.reshape(dp, tensor, norm_lines, model)
    tail = links.reduce(
        [jnp.concatenate([g_table[at], g_norms[:, at]], 1).reshape(-1, model) for at in spots], 0
    )
    tail_all = links.spread(tail)
    g_embed = tail_all[:, :share].reshape(-1, model)
    g_norm = tail_all[:, share:].reshape(tensor, -1)[:, :norm_share].reshape(-1)[:norm_size]
    g_norm = g_norm.reshape(norms, 2, depth)

    squares = jnp.sum(tail * tail) + jnp.sum(g_head * g_head)
    for group in (g_attend, g_expand, g_contract):
        for block in group:
            squares = squares + jnp.sum(block * block)
    grad_norm = jnp.sqrt(lax.psum(squares, ("dp", "tensor")))
    factor = clip_limit / jnp.maximum(grad_norm, clip_limit)

    g_in = jnp.stack([block[:, : 3 * part].reshape(depth, 3, part) for block in g_attend])
    g_out = jnp.stack([block[:, 3 * part :].T for block in g_attend])
    gradients = (
        g_in,
        g_out,
        jnp.stack(g_expand),
        jnp.stack([block.T for block in g_contract]),
        g_embed,
        g_head,
        g_norm,
    )
    params = (attend_in, attend_out, expand, contract, embed_table, logit_table, norm_params)
    moments_one = (
        attend_in_one,
        attend_out_one,
        expand_one,
        contract_one,
        embed_one,
        logit_one,
        norm_one,
    )
    moments_two = (
        attend_in_two,
        attend_out_two,
        expand_two,
        contract_two,
        embed_two,
        logit_two,
        norm_two,
    )
    results = []
    for index in range(7):
        rate_here = vector_rate if index == 6 else embed_rate if index == 4 else matrix_rate
        decay_here = 0.0 if index == 6 else weight_decay
        results.extend(
            adam_step(
                params[index],
                moments_one[index],
                moments_two[index],
                gradients[index],
                factor,
                rate_here,
                decay_here,
            )
        )
    return (*results, loss_sum, token_count, grad_norm)


def solution(mesh):
    in_specs = (
        (P("dp", None), P("dp"), P("dp", None))
        + (P(None, "dp", None, "tensor"),) * 3
        + (P(None, "tensor", "dp"),) * 3
        + (P(None, "dp", "tensor"),) * 3
        + (P(None, "tensor", "dp"),) * 3
        + (P("dp", None),) * 3
        + (P("dp", "tensor"),) * 3
        + (P(None, None, "dp"),) * 3
    )
    return jax.shard_map(
        functools.partial(body, mesh.shape["dp"], mesh.shape["tensor"]),
        mesh=mesh,
        in_specs=in_specs,
        out_specs=in_specs[3:] + (P(), P(), P()),
        check_vma=False,
    )
```

time: 1650 us -> 841 us (0.51)
  waiting for transfers between devices: 997 us -> 185 us
  Pallas kernels: 0 us -> 199 us
  blocking collectives: 180 us -> 65.4 us
  local copies, waits for them, and re-layouts: 188 us -> 133 us
  matrix products: 122 us -> 88.7 us
  starting transfers between devices: 2.09 us -> 33.1 us
  other arithmetic: 132 us -> 112 us
    unnamed x24 -> x0, waiting for transfers between devices: 337 us -> none
    psum x9 -> x0, waiting for transfers between devices: 326 us -> none  [the longest x5 204 us: input_total(): lax.psum(piece_sum.astype(jnp.bfloat16), 'tensor').astype(jnp.float32)]
    reduce_scatter x3 -> x0, waiting for transfers between devices: 224 us -> none  [the longest x1 129 us: body(): lax.psum_scatter(g_table, 'dp', scatter_dimension=0, tiled=True)]
    pallas_call x0 -> x5, Pallas kernels: none -> 199 us  [the longest x1 153 us: gather_all(): pl.pallas_call(functools.partial(gather_kernel, dims, shapes), out_shape=...]
    ppermute x0 -> x42, waiting for transfers between devices: none -> 185 us  [swap(): return lax.ppermute(value, axis, [(at, at ^ mask) for at in range(size)])]
    all_gather x4 -> x0, waiting for transfers between devices: 110 us -> none  [the longest x1 51.1 us: body(): lax.all_gather(expand.astype(jnp.bfloat16), 'dp', axis=1, tiled=True)]
    all_gather x3 -> x0, blocking collectives: 101 us -> none  [the longest x1 33.9 us: body(): lax.all_gather(norm_params.astype(jnp.bfloat16), 'dp', axis=2, tiled=True)]
    unnamed x365 -> x467, local copies, waits for them, and re-layouts: 94.6 us -> 33.3 us
  transfers between devices with their start and end apart: 20 -> 42, of which waited for: 18 -> 19; matrix products, arithmetic and copies ran while one was open for 12% -> 18% of each run, Pallas kernels for 0% -> 0%
where the time goes in v1:
time: 841 us; the launch traced here: 830 us
  Pallas kernels  199 us (24%)
  waiting for transfers between devices  185 us (22%)
  local copies, waits for them, and re-layouts  133 us (16%)
  other arithmetic  112 us (13%)
  matrix products  88.7 us (11%)
  blocking collectives  65.4 us (8%)
  starting transfers between devices  33.1 us (4%)
  between operations  13 us (2%)
    ppermute x42, waiting for transfers between devices, swap(): return lax.ppermute(value, axis, [(at, at ^ mask) for at in range(size)])  185 us
    pallas_call x1, Pallas kernels, gather_all(): pl.pallas_call(functools.partial(gather_kernel, dims, shapes), out_shape=...  153 us
    add x32, other arithmetic, reduce(): value = kept + self.swap(away.astype(kind_here), axis, mask).astype(full)  44.3 us
    dot_general x37, matrix products, matmul(): return jnp.dot(left, right, preferred_element_type=full)  43.6 us
    convert_element_type x35, local copies, waits for them, and re-layouts, reduce(): value = kept + self.swap(away.astype(kind_here), axis, mask).astype(full)  41.7 us
    psum x1, blocking collectives, body(): grad_norm = jnp.sqrt(lax.psum(squares, ('dp', 'tensor')))  39.4 us
    unnamed x467, local copies, waits for them, and re-layouts  33.3 us
    ppermute x42, starting transfers between devices, swap(): return lax.ppermute(value, axis, [(at, at ^ mask) for at in range(size)])  33.1 us
  transfers between devices with their start and end apart: 42, of which 19 were waited for; matrix products, arithmetic and copies ran while one was open for 18% of the time, Pallas kernels for 0%

profile of v1, /device:TPU:0, one launch (start us, length us, event | category | flops | bytes accessed | tf_op | source)
XLA Modules:
  0.0 829.6 jit_solution(16854121894593251659)
XLA Ops:
  8.7 152.8 %shard_map.415 = (bf16[2,2,4,2,80,768]{5,4,3,2,1,0:T(8,128)(2,1)}, bf16[2,2,4,2,96,768]{5,4,3,2,1,0:T(8,128)(2,1)}, bf16[2,2,4,2,96,768]{5,4,3,2,1,0:T(8,128)(2,...) custom-call(bf16[80,768]{1,0:T(8,128)(2,1)} %maximum_maximum_fusion., ...), custom_call_target="tpu_custom_call" | custom-call | tf_op jit(solution)/shard_map/pallas_call | solution.py:251
  167.7 2.7 fusion.224
  171.1 2.6 slice_bitcast_fusion.20
  176.0 9.4 %shard_map.416 = (bf16[257,192]{1,0:T(8,128)(2,1)S(1)}, bf16[257,192]{1,0:T(8,128)(2,1)S(1)}, bf16[257,192]{1,0:T(8,128)(2,1)S(1)}, bf16[257,192]{1,0:T(8,128)(2,1)S(1)}) custom-call(bf16[257,576]{1,0:T(8,128)(2,1)S(1)} %convolution_convert_fusion.7.refs_0_, bf16[257,576]{1,0:T(8,128)(2,1)S(1)} %convolution_convert_fusion.6.refs_1_, ...), custom_call_target="tpu_custom_call" | custom-call | flops 202902528 | bytes 1579008 | tf_op jit(solution)/shard_map/pallas_call | solution.py:78
  188.1 3.1 multiply_convert_fusion.5
  191.2 3.1 multiply_convert_fusion.6
  194.3 3.0 multiply_convert_fusion.7
  197.4 3.2 multiply_convert_fusion.8
  206.4 9.1 %shard_map.417 = (bf16[257,192]{1,0:T(8,128)(2,1)S(1)}, bf16[257,192]{1,0:T(8,128)(2,1)S(1)}, bf16[257,192]{1,0:T(8,128)(2,1)S(1)}, bf16[257,192]{1,0:T(8,128)(2,1)S(1)}) custom-call(bf16[257,576]{1,0:T(8,128)(2,1)S(1)} %convolution_convert_fusion.3.refs_0_, bf16[257,576]{1,0:T(8,128)(2,1)S(1)} %convolution_convert_fusion.2.refs_1_, ...), custom_call_target="tpu_custom_call" | custom-call | flops 202902528 | bytes 1579008 | tf_op jit(solution)/shard_map/pallas_call | solution.py:78
  218.2 3.2 multiply_convert_fusion.1
  221.4 3.1 multiply_convert_fusion.2
  224.5 3.1 multiply_convert_fusion.3
  227.6 3.1 multiply_convert_fusion.4
  238.1 26.0 %psum.21 = f32[]{:T(128)} all-reduce(f32[]{:T(128)} %convert_reduce_fusion), channel_id=1, replica_groups=mesh['dp'=8,'tensor'=4] {'dp'}, use_global_device_ids=true, to_apply=%region_16.17 | all-reduce | flops 1 | bytes 8 | tf_op jit(solution)/shard_map/psum | solution.py:397
  283.7 13.9 %shard_map.418 = (bf16[257,576]{1,0:T(8,128)(2,1)S(1)}, bf16[257,576]{1,0:T(8,128)(2,1)S(1)}, bf16[257,576]{1,0:T(8,128)(2,1)S(1)}, bf16[257,576]{1,0:T(8,128)(2,1)S(1)}) custom-call(bf16[257,576]{1,0:T(8,128)(2,1)S(1)} %convolution_convert_fusion.3.refs_0_, bf16[257,576]{1,0:T(8,128)(2,1)S(1)} %convolution_convert_fusion.2.refs_1_, ...), custom_call_target="tpu_custom_call" | custom-call | flops 507256320 | bytes 2763264 | tf_op jit(solution)/shard_map/pallas_call | solution.py:116
  315.3 14.0 %shard_map.419 = (bf16[257,576]{1,0:T(8,128)(2,1)S(1)}, bf16[257,576]{1,0:T(8,128)(2,1)S(1)}, bf16[257,576]{1,0:T(8,128)(2,1)S(1)}, bf16[257,576]{1,0:T(8,128)(2,1)S(1)}) custom-call(bf16[257,576]{1,0:T(8,128)(2,1)S(1)} %copy-done.15, bf16[257,576]{1,0:T(8,128)(2,1)S(1)} %copy-done.13, bf16[257,576]{1,0:T(8,128)(2,1)S(1)} %copy-done.11, ...), custom_call_target="tpu_custom_call" | custom-call | flops 507256320 | bytes 2763264 | tf_op jit(solution)/shard_map/pallas_call | solution.py:116
  332.3 3.0 fusion.8
  335.3 3.0 fusion.222
  339.5 3.0 pad_maximum_fusion.8
  342.5 3.1 stack_reshape.20
  345.6 3.0 pad_maximum_fusion.9
  348.6 3.1 stack_reshape.21
  351.7 3.0 pad_maximum_fusion.10
  354.7 3.2 stack_reshape.22
  357.9 3.0 pad_maximum_fusion.11
  360.9 3.1 stack_reshape.23
  364.0 5.2 pad_maximum_fusion.6
  369.2 6.7 reshape.537
  378.3 2.7 copy.177
  415.7 3.9 pad_maximum_fusion.1
  419.6 3.9 pad_maximum_fusion
  424.6 9.6 %copy.174 = f32[4,768,768]{2,1,0:T(8,128)} copy(f32[4,768,768]{1,2,0:T(8,128)} %pad_maximum_fusion.1) | data formatting | bytes 18874368 | tf_op jit(solution)/shard_map/stack | solution.py:302
  434.2 9.9 %copy.172 = f32[4,768,768]{2,1,0:T(8,128)} copy(f32[4,768,768]{1,2,0:T(8,128)} %pad_maximum_fusion) | data formatting | bytes 18874368 | tf_op jit(solution)/shard_map/stack | solution.py:302
  458.0 7.4 collective-permute-done.16
  465.9 5.8 collective-permute-done.17
  471.9 4.2 fusion.13
  476.6 4.2 fusion.12
  483.9 7.1 bitcast_add_fusion.6
  491.0 3.0 fusion.49
  494.1 4.8 bitcast_add_fusion
  499.8 2.4 bitcast_add_fusion.1
  502.3 4.6 fusion.28
  508.4 4.8 bitcast_add_fusion.2
  517.2 2.8 fusion.26
  522.4 2.6 bitcast_add_fusion.4
  526.1 2.9 bitcast_add_fusion.13
  531.1 2.5 bitcast_add_fusion.5
  534.4 36.8 %collective-permute-done.12 = bf16[2,2,73,768]{3,1,2,0:T(2,128)(2,1)S(1)} collective-permute-done((bf16[2,2,73,768]{3,1,2,0:T(2,128)(2,1)S(1)}, bf16[2,2,73,768]{3,1,2,0:T(2,128)(2,1)S(1)}, u32[]{:S(2)}, u32[]{:S(2)}) %collective-permute-start.12) | collective-permute-done | bytes 448544 | tf_op jit(solution)/shard_map/ppermute | solution.py:297
  574.7 4.7 collective-permute-done.13
  597.1 11.2 %collective-permute-done.6 = bf16[2,2,2,96,768]{4,3,2,1,0:T(8,128)(2,1)S(1)} collective-permute-done((bf16[2,2,2,96,768]{4,3,2,1,0:T(8,128)(2,1)S(1)}, bf16[2,2,2,96,768]{4,3,2,1,0:T(8,128)(2,1)S(1)}, u32[]{:S(2)}, u32[]{:S(2)}) %collective-permute-start.6) | collective-permute-done | bytes 1179680 | tf_op jit(solution)/shard_map/ppermute | solution.py:297
  608.9 24.7 %collective-permute-done.1 = bf16[2,2,2,96,768]{4,3,2,1,0:T(8,128)(2,1)S(1)} collective-permute-done((bf16[2,2,2,96,768]{4,3,2,1,0:T(8,128)(2,1)S(1)}, bf16[2,2,2,96,768]{4,3,2,1,0:T(8,128)(2,1)S(1)}, u32[]{:S(2)}, u32[]{:S(2)}) %collective-permute-start.1) | collective-permute-done | bytes 1179680 | tf_op jit(solution)/shard_map/ppermute | solution.py:297
  643.2 3.2 collective-permute-done.27
  649.3 7.3 collective-permute-done.22
  660.0 6.4 collective-permute-done.2
  668.2 8.1 collective-permute-done.41
  683.7 13.6 %collective-permute-done.8 = bf16[2,96,768]{2,1,0:T(8,128)(2,1)S(1)} collective-permute-done((bf16[2,96,768]{2,1,0:T(8,128)(2,1)S(1)}, bf16[2,96,768]{2,1,0:T(8,128)(2,1)S(1)}, u32[]{:S(2)}, u32[]{:S(2)}) %collective-permute-start.8) | collective-permute-done | bytes 294944 | tf_op jit(solution)/shard_map/ppermute | solution.py:297
  697.8 4.3 collective-permute-done.3
  702.7 28.0 %collective-permute-done.34 = f32[96,768]{1,0:T(8,128)S(1)} collective-permute-done((f32[96,768]{1,0:T(8,128)S(1)}, f32[96,768]{1,0:T(8,128)S(1)}, u32[]{:S(2)}, u32[]{:S(2)}) %collective-permute-start.34) | collective-permute-done | bytes 294944 | tf_op jit(solution)/shard_map/ppermute | solution.py:297
  732.0 8.1 collective-permute-done.29
  741.5 5.0 collective-permute-done.24
  747.8 5.0 collective-permute-done.9
  753.5 3.6 collective-permute-done.4
  765.2 39.4 %all-reduce.2 = (f32[]{:T(128)}, f32[]{:T(128)}) all-reduce(f32[]{:T(128)S(6)} %add.834, f32[]{:T(128)} %get-tuple-element.266), channel_id=1, replica_groups=mesh['dp'=8,'tensor'=4] {'dp','tensor'}, use_global_device_ids=true, to_apply=%region_45.46 | all-reduce | flops 2 | bytes 16 | tf_op jit(solution)/shard_map/psum | solution.py:517
  820.8 3.5 multiply_subtract_fusion
  (858 shorter events, 216.3 us)
Async XLA Ops:
  170.4 16.3 %copy-start.24 = (f32[257,768]{1,0:T(8,128)}, f32[257,768]{1,0:T(8,128)S(1)}, u32[]{:S(2)}) copy-start(f32[257,768]{1,0:T(8,128)S(1)} %get-tuple-element.357) | copy-start | bytes 2368516
  187.3 15.2 %copy-start.26 = (f32[257,768]{1,0:T(8,128)}, f32[257,768]{1,0:T(8,128)S(1)}, u32[]{:S(2)}) copy-start(f32[257,768]{1,0:T(8,128)S(1)} %get-tuple-element.359) | copy-start | bytes 2368516
  203.2 14.0 %copy-start.18 = (f32[257,768]{1,0:T(8,128)}, f32[257,768]{1,0:T(8,128)S(1)}, u32[]{:S(2)}) copy-start(f32[257,768]{1,0:T(8,128)S(1)} %get-tuple-element.365) | copy-start | bytes 2368516
  217.7 14.9 %copy-start.28 = (f32[257,768]{1,0:T(8,128)}, f32[257,768]{1,0:T(8,128)S(1)}, u32[]{:S(2)}) copy-start(f32[257,768]{1,0:T(8,128)S(1)} %get-tuple-element.367) | copy-start | bytes 2368516
  233.8 32.3 %copy-start.16 = (bf16[257,768]{1,0:T(8,128)(2,1)}, bf16[257,768]{1,0:T(8,128)(2,1)S(1)}, u32[]{:S(2)}) copy-start(bf16[257,768]{1,0:T(8,128)(2,1)S(1)} %add_convert_fusion.9) | copy-start | bytes 1184260
  233.8 30.3 %copy-start.164 = (s32[1,256]{1,0:T(1,128)S(1)}, s32[1,256]{1,0:T(1,128)}, u32[]{:S(2)}) copy-start(s32[1,256]{1,0:T(1,128)} %get-tuple-element.305) | copy-start | bytes 3076
  233.8 30.4 %copy-start.163 = (f32[1,256]{1,0:T(1,128)S(1)}, f32[1,256]{1,0:T(1,128)}, u32[]{:S(2)}) copy-start(f32[1,256]{1,0:T(1,128)} %get-tuple-element.354) | copy-start | bytes 3076
  381.0 102.4 %collective-permute-start.10 = (bf16[2,2,2,2,73,768]{5,3,4,2,1,0:T(2,128)(2,1)}, bf16[2,2,2,2,73,768]{5,3,4,2,1,0:T(2,128)(2,1)}, u32[]{:S(2)}, u32[]{:S(2)}) collective-permute-start(bf16[2,2,2,2,73,768]{5,3,4,2,1,0:T(2,128)(2,1)} %copy.177), channel_id=1, source_target_pairs={{0,1},{1,0},{2,3},{3,2},{4,5},{5,4},{6,7},{7,6},{8,9},{9,8},{10,11... | collective-permute-start | bytes 5382152 | tf_op jit(solution)/shard_map/ppermute | solution.py:297
  387.4 106.6 %collective-permute-start.35 = (bf16[2,2,2,2,96,768]{5,4,3,2,1,0:T(8,128)(2,1)}, bf16[2,2,2,2,96,768]{5,4,3,2,1,0:T(8,128)(2,1)}, u32[]{:S(2)}, u32[]{:S(2)}) collective-permute-start(bf16[2,2,2,2,96,768]{5,4,3,2,1,0:T(8,128)(2,1)} %fusion.17), channel_id=1, source_target_pairs={{0,1},{1,0},{2,3},{3,2},{4,5},{5,4},{6,7},{7,6},{8,9},{9,8},{10,11... | collective-permute-start | bytes 7077896 | tf_op jit(solution)/shard_map/ppermute | solution.py:297
  394.4 104.5 %collective-permute-start.30 = (bf16[2,2,2,2,96,768]{5,4,3,2,1,0:T(8,128)(2,1)}, bf16[2,2,2,2,96,768]{5,4,3,2,1,0:T(8,128)(2,1)}, u32[]{:S(2)}, u32[]{:S(2)}) collective-permute-start(bf16[2,2,2,2,96,768]{5,4,3,2,1,0:T(8,128)(2,1)} %fusion.16), channel_id=1, source_target_pairs={{0,1},{1,0},{2,3},{3,2},{4,5},{5,4},{6,7},{7,6},{8,9},{9,8},{10,11... | collective-permute-start | bytes 7077896 | tf_op jit(solution)/shard_map/ppermute | solution.py:297
  402.1 106.0 %collective-permute-start.25 = (bf16[2,2,2,2,96,768]{5,4,3,2,1,0:T(8,128)(2,1)}, bf16[2,2,2,2,96,768]{5,4,3,2,1,0:T(8,128)(2,1)}, u32[]{:S(2)}, u32[]{:S(2)}) collective-permute-start(bf16[2,2,2,2,96,768]{5,4,3,2,1,0:T(8,128)(2,1)} %fusion.15), channel_id=1, source_target_pairs={{0,1},{1,0},{2,3},{3,2},{4,5},{5,4},{6,7},{7,6},{8,9},{9,8},{10,11... | collective-permute-start | bytes 7077896 | tf_op jit(solution)/shard_map/ppermute | solution.py:297
  405.6 45.9 %collective-permute-start.15 = (bf16[2,2,2,2,96,256]{5,4,3,2,1,0:T(8,128)(2,1)}, bf16[2,2,2,2,96,256]{5,4,3,2,1,0:T(8,128)(2,1)}, u32[]{:S(2)}, u32[]{:S(2)}) collective-permute-start(bf16[2,2,2,2,96,256]{5,4,3,2,1,0:T(8,128)(2,1)} %fusion.121), channel_id=1, source_target_pairs={{0,1},{1,0},{2,3},{3,2},{4,5},{5,4},{6,7},{7,6},{8,9},{9,8},{10,11... | collective-permute-start | bytes 2359304 | tf_op jit(solution)/shard_map/ppermute | solution.py:297
  454.2 11.2 %collective-permute-start.16 = (bf16[2,2,2,96,256]{4,3,2,1,0:T(8,128)(2,1)S(1)}, bf16[2,2,2,96,256]{4,3,2,1,0:T(8,128)(2,1)S(1)}, u32[]{:S(2)}, u32[]{:S(2)}) collective-permute-start(bf16[2,2,2,96,256]{4,3,2,1,0:T(8,128)(2,1)S(1)} %fusion.131), channel_id=1, source_target_pairs={{0,2},{1,3},{2,0},{3,1},{4,6},{5,7},{6,4},{7,5},{8,10},{9,11},{10,... | collective-permute-start | bytes 1179656 | tf_op jit(solution)/shard_map/ppermute | solution.py:297
  465.5 6.2 collective-permute-start.17
  471.8 4.7 collective-permute-start.18
  471.9 22.2 %slice-start = ((s8[9437184]{0:T(1024)(128)(4,1)}), s8[4194304]{0:T(1024)(128)(4,1)S(1)}, s32[]{:S(2)}) async-start(s8[9437184]{0:T(1024)(128)(4,1)} %bitcast.638), calls=%async_computation | async-start | bytes 8388608
  476.5 5.6 collective-permute-start.19
  476.6 17.4 %slice-start.1 = ((s8[9437184]{0:T(1024)(128)(4,1)}), s8[4194304]{0:T(1024)(128)(4,1)S(1)}, s32[]{:S(2)}) async-start(s8[9437184]{0:T(1024)(128)(4,1)} %bitcast.638), calls=%async_computation.1 | async-start | bytes 8388608
  482.1 31.1 %collective-permute-start.20 = (bf16[2,2,2,2,96,768]{5,4,3,2,1,0:T(8,128)(2,1)}, bf16[2,2,2,2,96,768]{5,4,3,2,1,0:T(8,128)(2,1)}, u32[]{:S(2)}, u32[]{:S(2)}) collective-permute-start(bf16[2,2,2,2,96,768]{5,4,3,2,1,0:T(8,128)(2,1)} %fusion.14), channel_id=1, source_target_pairs={{0,1},{1,0},{2,3},{3,2},{4,5},{5,4},{6,7},{7,6},{8,9},{9,8},{10,11... | collective-permute-start | bytes 7077896 | tf_op jit(solution)/shard_map/ppermute | solution.py:297
  483.4 37.8 %collective-permute-start.5 = (bf16[2,2,2,2,96,768]{5,4,3,2,1,0:T(8,128)(2,1)}, bf16[2,2,2,2,96,768]{5,4,3,2,1,0:T(8,128)(2,1)}, u32[]{:S(2)}, u32[]{:S(2)}) collective-permute-start(bf16[2,2,2,2,96,768]{5,4,3,2,1,0:T(8,128)(2,1)} %fusion.13), channel_id=1, source_target_pairs={{0,1},{1,0},{2,3},{3,2},{4,5},{5,4},{6,7},{7,6},{8,9},{9,8},{10,11... | collective-permute-start | bytes 7077896 | tf_op jit(solution)/shard_map/ppermute | solution.py:297
  483.9 15.9 %slice-start.3 = ((s8[9437184]{0:T(1024)(128)(4,1)}), s8[4194304]{0:T(1024)(128)(4,1)S(1)}, s32[]{:S(2)}) async-start(s8[9437184]{0:T(1024)(128)(4,1)} %bitcast.642), calls=%async_computation.3 | async-start | bytes 8388608
  483.9 15.9 %slice-start.4 = ((s8[9437184]{0:T(1024)(128)(4,1)}), s8[4194304]{0:T(1024)(128)(4,1)S(1)}, s32[]{:S(2)}) async-start(s8[9437184]{0:T(1024)(128)(4,1)} %bitcast.642), calls=%async_computation.4 | async-start | bytes 8388608
  494.0 36.5 %collective-permute-start = (bf16[2,2,2,2,96,768]{5,4,3,2,1,0:T(8,128)(2,1)}, bf16[2,2,2,2,96,768]{5,4,3,2,1,0:T(8,128)(2,1)}, u32[]{:S(2)}, u32[]{:S(2)}) collective-permute-start(bf16[2,2,2,2,96,768]{5,4,3,2,1,0:T(8,128)(2,1)} %fusion.12), channel_id=1, source_target_pairs={{0,1},{1,0},{2,3},{3,2},{4,5},{5,4},{6,7},{7,6},{8,9},{9,8},{10,11... | collective-permute-start | bytes 7077896 | tf_op jit(solution)/shard_map/ppermute | solution.py:297
  494.0 14.3 %slice-start.6 = ((s8[9437184]{0:T(1024)(128)(4,1)}), s8[4194304]{0:T(1024)(128)(4,1)S(1)}, s32[]{:S(2)}) async-start(s8[9437184]{0:T(1024)(128)(4,1)} %bitcast.646), calls=%async_computation.6 | async-start | bytes 8388608
  494.1 14.3 %slice-start.7 = ((s8[9437184]{0:T(1024)(128)(4,1)}), s8[4194304]{0:T(1024)(128)(4,1)S(1)}, s32[]{:S(2)}) async-start(s8[9437184]{0:T(1024)(128)(4,1)} %bitcast.646), calls=%async_computation.7 | async-start | bytes 8388608
  498.9 26.2 %collective-permute-start.11 = (bf16[2,2,2,73,768]{4,2,3,1,0:T(2,128)(2,1)}, bf16[2,2,2,73,768]{4,2,3,1,0:T(2,128)(2,1)}, u32[]{:S(2)}, u32[]{:S(2)}) collective-permute-start(bf16[2,2,2,73,768]{4,2,3,1,0:T(2,128)(2,1)} %fusion.49), channel_id=1, source_target_pairs={{0,2},{1,3},{2,0},{3,1},{4,6},{5,7},{6,4},{7,5},{8,10},{9,11},{10,... | collective-permute-start | bytes 2691080 | tf_op jit(solution)/shard_map/ppermute | solution.py:297
  499.8 15.1 %slice-start.15 = ((s8[9437184]{0:T(1024)(128)(4,1)}), s8[1048576]{0:T(1024)(128)(4,1)S(1)}, s32[]{:S(2)}) async-start(s8[9437184]{0:T(1024)(128)(4,1)} %bitcast.658), calls=%async_computation.15 | async-start | bytes 2097152
  499.8 15.1 %slice-start.16 = ((s8[9437184]{0:T(1024)(128)(4,1)}), s8[4194304]{0:T(1024)(128)(4,1)S(1)}, s32[]{:S(2)}) async-start(s8[9437184]{0:T(1024)(128)(4,1)} %bitcast.658), calls=%async_computation.16 | async-start | bytes 8388608
  508.0 72.5 %collective-permute-start.36 = (bf16[2,2,2,96,768]{4,3,2,1,0:T(8,128)(2,1)}, bf16[2,2,2,96,768]{4,3,2,1,0:T(8,128)(2,1)}, u32[]{:S(2)}, u32[]{:S(2)}) collective-permute-start(bf16[2,2,2,96,768]{4,3,2,1,0:T(8,128)(2,1)} %fusion.28), channel_id=1, source_target_pairs={{0,4},{4,0},{8,12},{12,8},{16,20},{20,16},{24,28},{28,24},{1,5},{5... | collective-permute-start | bytes 3538952 | tf_op jit(solution)/shard_map/ppermute | solution.py:297
  508.4 14.0 %slice-start.12 = ((s8[9437184]{0:T(1024)(128)(4,1)}), s8[1048576]{0:T(1024)(128)(4,1)S(1)}, s32[]{:S(2)}) async-start(s8[9437184]{0:T(1024)(128)(4,1)} %bitcast.654), calls=%async_computation.12 | async-start | bytes 2097152
  513.2 70.9 %collective-permute-start.31 = (bf16[2,2,2,96,768]{4,3,2,1,0:T(8,128)(2,1)}, bf16[2,2,2,96,768]{4,3,2,1,0:T(8,128)(2,1)}, u32[]{:S(2)}, u32[]{:S(2)}) collective-permute-start(bf16[2,2,2,96,768]{4,3,2,1,0:T(8,128)(2,1)} %fusion.27), channel_id=1, source_target_pairs={{0,4},{4,0},{8,12},{12,8},{16,20},{20,16},{24,28},{28,24},{1,5},{5... | collective-permute-start | bytes 3538952 | tf_op jit(solution)/shard_map/ppermute | solution.py:297
  521.2 68.1 %collective-permute-start.26 = (bf16[2,2,2,96,768]{4,3,2,1,0:T(8,128)(2,1)}, bf16[2,2,2,96,768]{4,3,2,1,0:T(8,128)(2,1)}, u32[]{:S(2)}, u32[]{:S(2)}) collective-permute-start(bf16[2,2,2,96,768]{4,3,2,1,0:T(8,128)(2,1)} %fusion.26), channel_id=1, source_target_pairs={{0,2},{1,3},{2,0},{3,1},{4,6},{5,7},{6,4},{7,5},{8,10},{9,11},{10,... | collective-permute-start | bytes 3538952 | tf_op jit(solution)/shard_map/ppermute | solution.py:297
  525.1 67.9 %collective-permute-start.21 = (bf16[2,2,2,96,768]{4,3,2,1,0:T(8,128)(2,1)}, bf16[2,2,2,96,768]{4,3,2,1,0:T(8,128)(2,1)}, u32[]{:S(2)}, u32[]{:S(2)}) collective-permute-start(bf16[2,2,2,96,768]{4,3,2,1,0:T(8,128)(2,1)} %fusion.25), channel_id=1, source_target_pairs={{0,2},{1,3},{2,0},{3,1},{4,6},{5,7},{6,4},{7,5},{8,10},{9,11},{10,... | collective-permute-start | bytes 3538952 | tf_op jit(solution)/shard_map/ppermute | solution.py:297
  529.8 52.5 %slice-start.20 = ((s8[4718592]{0:T(1024)(128)(4,1)}), s8[4194304]{0:T(1024)(128)(4,1)S(1)}, s32[]{:S(2)}) async-start(s8[4718592]{0:T(1024)(128)(4,1)} %bitcast.663), calls=%async_computation.20 | async-start | bytes 8388608
  530.5 51.8 %slice-start.21 = ((s8[4718592]{0:T(1024)(128)(4,1)}), s8[524288]{0:T(1024)(128)(4,1)S(1)}, s32[]{:S(2)}) async-start(s8[4718592]{0:T(1024)(128)(4,1)} %bitcast.663), calls=%async_computation.21 | async-start | bytes 1048576
  530.5 40.7 %collective-permute-start.12 = (bf16[2,2,73,768]{3,1,2,0:T(2,128)(2,1)S(1)}, bf16[2,2,73,768]{3,1,2,0:T(2,128)(2,1)S(1)}, u32[]{:S(2)}, u32[]{:S(2)}) collective-permute-start(bf16[2,2,73,768]{3,1,2,0:T(2,128)(2,1)S(1)} %bitcast.747), channel_id=1, source_target_pairs={{0,4},{4,0},{8,12},{12,8},{16,20},{20,16},{24,28},{28,24},{1,5},{5... | collective-permute-start | bytes 1345544 | tf_op jit(solution)/shard_map/ppermute | solution.py:297
  571.3 14.6 %slice-start.22 = ((s8[4718592]{0:T(1024)(128)(4,1)}), s8[4194304]{0:T(1024)(128)(4,1)S(1)}, s32[]{:S(2)}) async-start(s8[4718592]{0:T(1024)(128)(4,1)} %bitcast.665), calls=%async_computation.22 | async-start | bytes 8388608
  572.5 6.9 collective-permute-start.13
  579.5 28.9 %collective-permute-start.6 = (bf16[2,2,2,96,768]{4,3,2,1,0:T(8,128)(2,1)S(1)}, bf16[2,2,2,96,768]{4,3,2,1,0:T(8,128)(2,1)S(1)}, u32[]{:S(2)}, u32[]{:S(2)}) collective-permute-start(bf16[2,2,2,96,768]{4,3,2,1,0:T(8,128)(2,1)S(1)} %fusion.24), channel_id=1, source_target_pairs={{0,4},{4,0},{8,12},{12,8},{16,20},{20,16},{24,28},{28,24},{1,5},{5... | collective-permute-start | bytes 3538952 | tf_op jit(solution)/shard_map/ppermute | solution.py:297
  580.5 53.1 %collective-permute-start.1 = (bf16[2,2,2,96,768]{4,3,2,1,0:T(8,128)(2,1)S(1)}, bf16[2,2,2,96,768]{4,3,2,1,0:T(8,128)(2,1)S(1)}, u32[]{:S(2)}, u32[]{:S(2)}) collective-permute-start(bf16[2,2,2,96,768]{4,3,2,1,0:T(8,128)(2,1)S(1)} %fusion.23), channel_id=1, source_target_pairs={{0,4},{4,0},{8,12},{12,8},{16,20},{20,16},{24,28},{28,24},{1,5},{5... | collective-permute-start | bytes 3538952 | tf_op jit(solution)/shard_map/ppermute | solution.py:297
  584.1 50.1 %collective-permute-start.14 = (f32[73,768]{1,0:T(8,128)S(1)}, f32[73,768]{1,0:T(8,128)S(1)}, u32[]{:S(2)}, u32[]{:S(2)}) collective-permute-start(f32[73,768]{1,0:T(8,128)S(1)} %bitcast.748), channel_id=1, source_target_pairs={{0,16},{4,20},{8,24},{12,28},{16,0},{20,4},{24,8},{28,12},{1,17},{... | collective-permute-start | bytes 672776 | tf_op jit(solution)/shard_map/ppermute | solution.py:297
  589.3 49.3 %collective-permute-start.37 = (bf16[2,2,96,768]{3,2,1,0:T(8,128)(2,1)}, bf16[2,2,96,768]{3,2,1,0:T(8,128)(2,1)}, u32[]{:S(2)}, u32[]{:S(2)}) collective-permute-start(bf16[2,2,96,768]{3,2,1,0:T(8,128)(2,1)} %fusion.130), channel_id=1, source_target_pairs={{0,2},{1,3},{2,0},{3,1},{4,6},{5,7},{6,4},{7,5},{8,10},{9,11},{10,... | collective-permute-start | bytes 1769480 | tf_op jit(solution)/shard_map/ppermute | solution.py:297
  593.7 47.0 %collective-permute-start.32 = (bf16[2,2,96,768]{3,2,1,0:T(8,128)(2,1)}, bf16[2,2,96,768]{3,2,1,0:T(8,128)(2,1)}, u32[]{:S(2)}, u32[]{:S(2)}) collective-permute-start(bf16[2,2,96,768]{3,2,1,0:T(8,128)(2,1)} %fusion.129), channel_id=1, source_target_pairs={{0,2},{1,3},{2,0},{3,1},{4,6},{5,7},{6,4},{7,5},{8,10},{9,11},{10,... | collective-permute-start | bytes 1769480 | tf_op jit(solution)/shard_map/ppermute | solution.py:297
  608.4 38.0 %collective-permute-start.27 = (bf16[2,2,96,768]{3,2,1,0:T(8,128)(2,1)}, bf16[2,2,96,768]{3,2,1,0:T(8,128)(2,1)}, u32[]{:S(2)}, u32[]{:S(2)}) collective-permute-start(bf16[2,2,96,768]{3,2,1,0:T(8,128)(2,1)} %fusion.128), channel_id=1, source_target_pairs={{0,4},{4,0},{8,12},{12,8},{16,20},{20,16},{24,28},{28,24},{1,5},{5... | collective-permute-start | bytes 1769480 | tf_op jit(solution)/shard_map/ppermute | solution.py:297
  608.9 26.0 %copy-start.58 = (f32[2,2,2,96,768]{4,3,2,1,0:T(8,128)}, f32[2,2,2,96,768]{4,3,2,1,0:T(8,128)S(1)}, u32[]{:S(2)}) copy-start(f32[2,2,2,96,768]{4,3,2,1,0:T(8,128)S(1)} %bitcast_add_fusion.11) | copy-start | bytes 7077892
  633.7 22.9 %collective-permute-start.22 = (bf16[2,2,96,768]{3,2,1,0:T(8,128)(2,1)}, bf16[2,2,96,768]{3,2,1,0:T(8,128)(2,1)}, u32[]{:S(2)}, u32[]{:S(2)}) collective-permute-start(bf16[2,2,96,768]{3,2,1,0:T(8,128)(2,1)} %fusion.127), channel_id=1, source_target_pairs={{0,4},{4,0},{8,12},{12,8},{16,20},{20,16},{24,28},{28,24},{1,5},{5... | collective-permute-start | bytes 1769480 | tf_op jit(solution)/shard_map/ppermute | solution.py:297
  634.9 2.4 collective-permute-start.40
  637.3 22.1 %collective-permute-start.7 = (bf16[2,2,96,768]{3,2,1,0:T(8,128)(2,1)}, bf16[2,2,96,768]{3,2,1,0:T(8,128)(2,1)S(1)}, u32[]{:S(2)}, u32[]{:S(2)}) collective-permute-start(bf16[2,2,96,768]{3,2,1,0:T(8,128)(2,1)} %fusion.126), channel_id=1, source_target_pairs={{0,2},{1,3},{2,0},{3,1},{4,6},{5,7},{6,4},{7,5},{8,10},{9,11},{10,... | collective-permute-start | bytes 1769480 | tf_op jit(solution)/shard_map/ppermute | solution.py:297
  638.6 27.8 %collective-permute-start.2 = (bf16[2,2,96,768]{3,2,1,0:T(8,128)(2,1)S(1)}, bf16[2,2,96,768]{3,2,1,0:T(8,128)(2,1)S(1)}, u32[]{:S(2)}, u32[]{:S(2)}) collective-permute-start(bf16[2,2,96,768]{3,2,1,0:T(8,128)(2,1)S(1)} %fusion.125), channel_id=1, source_target_pairs={{0,2},{1,3},{2,0},{3,1},{4,6},{5,7},{6,4},{7,5},{8,10},{9,11},{10,... | collective-permute-start | bytes 1769480 | tf_op jit(solution)/shard_map/ppermute | solution.py:297
  640.7 35.6 %collective-permute-start.41 = (f32[2,73,768]{2,1,0:T(8,128)S(1)}, f32[2,73,768]{2,1,0:T(8,128)S(1)}, u32[]{:S(2)}, u32[]{:S(2)}) collective-permute-start(f32[2,73,768]{2,1,0:T(8,128)S(1)} %maximum_select_fusion.1), channel_id=1, source_target_pairs={{0,2},{1,3},{2,0},{3,1},{4,6},{5,7},{6,4},{7,5},{8,10},{9,11},{10,... | collective-permute-start | bytes 1345544 | tf_op jit(solution)/shard_map/ppermute | solution.py:297
  643.1 15.0 %copy-start.51 = (f32[2,2,2,96,768]{4,3,2,1,0:T(8,128)S(1)}, f32[2,2,2,96,768]{4,3,2,1,0:T(8,128)}, u32[]{:S(2)}) copy-start(f32[2,2,2,96,768]{4,3,2,1,0:T(8,128)} %copy-done.50) | copy-start | bytes 7077892
  646.4 31.7 %collective-permute-start.38 = (bf16[2,96,768]{2,1,0:T(8,128)(2,1)S(1)}, bf16[2,96,768]{2,1,0:T(8,128)(2,1)S(1)}, u32[]{:S(2)}, u32[]{:S(2)}) collective-permute-start(bf16[2,96,768]{2,1,0:T(8,128)(2,1)S(1)} %fusion.160), channel_id=1, source_target_pairs={{0,8},{4,12},{8,0},{12,4},{16,24},{20,28},{24,16},{28,20},{1,9},{5... | collective-permute-start | bytes 884744 | tf_op jit(solution)/shard_map/ppermute | solution.py:297
  656.6 22.1 %collective-permute-start.33 = (bf16[2,96,768]{2,1,0:T(8,128)(2,1)S(1)}, bf16[2,96,768]{2,1,0:T(8,128)(2,1)S(1)}, u32[]{:S(2)}, u32[]{:S(2)}) collective-permute-start(bf16[2,96,768]{2,1,0:T(8,128)(2,1)S(1)} %fusion.159), channel_id=1, source_target_pairs={{0,8},{4,12},{8,0},{12,4},{16,24},{20,28},{24,16},{28,20},{1,9},{5... | collective-permute-start | bytes 884744 | tf_op jit(solution)/shard_map/ppermute | solution.py:297
  659.4 21.0 %collective-permute-start.28 = (bf16[2,96,768]{2,1,0:T(8,128)(2,1)S(1)}, bf16[2,96,768]{2,1,0:T(8,128)(2,1)S(1)}, u32[]{:S(2)}, u32[]{:S(2)}) collective-permute-start(bf16[2,96,768]{2,1,0:T(8,128)(2,1)S(1)} %fusion.158), channel_id=1, source_target_pairs={{0,8},{4,12},{8,0},{12,4},{16,24},{20,28},{24,16},{28,20},{1,9},{5... | collective-permute-start | bytes 884744 | tf_op jit(solution)/shard_map/ppermute | solution.py:297
  666.4 15.5 %collective-permute-start.23 = (bf16[2,96,768]{2,1,0:T(8,128)(2,1)S(1)}, bf16[2,96,768]{2,1,0:T(8,128)(2,1)S(1)}, u32[]{:S(2)}, u32[]{:S(2)}) collective-permute-start(bf16[2,96,768]{2,1,0:T(8,128)(2,1)S(1)} %fusion.157), channel_id=1, source_target_pairs={{0,8},{4,12},{8,0},{12,4},{16,24},{20,28},{24,16},{28,20},{1,9},{5... | collective-permute-start | bytes 884744 | tf_op jit(solution)/shard_map/ppermute | solution.py:297
  676.4 21.0 %collective-permute-start.8 = (bf16[2,96,768]{2,1,0:T(8,128)(2,1)S(1)}, bf16[2,96,768]{2,1,0:T(8,128)(2,1)S(1)}, u32[]{:S(2)}, u32[]{:S(2)}) collective-permute-start(bf16[2,96,768]{2,1,0:T(8,128)(2,1)S(1)} %fusion.156), channel_id=1, source_target_pairs={{0,8},{4,12},{8,0},{12,4},{16,24},{20,28},{24,16},{28,20},{1,9},{5... | collective-permute-start | bytes 884744 | tf_op jit(solution)/shard_map/ppermute | solution.py:297
  678.1 24.1 %collective-permute-start.3 = (bf16[2,96,768]{2,1,0:T(8,128)(2,1)S(1)}, bf16[2,96,768]{2,1,0:T(8,128)(2,1)S(1)}, u32[]{:S(2)}, u32[]{:S(2)}) collective-permute-start(bf16[2,96,768]{2,1,0:T(8,128)(2,1)S(1)} %fusion.155), channel_id=1, source_target_pairs={{0,8},{4,12},{8,0},{12,4},{16,24},{20,28},{24,16},{28,20},{1,9},{5... | collective-permute-start | bytes 884744 | tf_op jit(solution)/shard_map/ppermute | solution.py:297
  678.7 84.6 %collective-permute-start.39 = (f32[96,768]{1,0:T(8,128)S(1)}, f32[96,768]{1,0:T(8,128)S(1)}, u32[]{:S(2)}, u32[]{:S(2)}) collective-permute-start(f32[96,768]{1,0:T(8,128)S(1)} %dynamic-slice_bitcast_fusion), channel_id=1, source_target_pairs={{0,16},{4,20},{8,24},{12,28},{16,0},{20,4},{24,8},{28,12},{1,17},{... | collective-permute-start | bytes 884744 | tf_op jit(solution)/shard_map/ppermute | solution.py:297
  680.5 50.2 %collective-permute-start.34 = (f32[96,768]{1,0:T(8,128)S(1)}, f32[96,768]{1,0:T(8,128)S(1)}, u32[]{:S(2)}, u32[]{:S(2)}) collective-permute-start(f32[96,768]{1,0:T(8,128)S(1)} %dynamic-slice_bitcast_fusion.1), channel_id=1, source_target_pairs={{0,16},{4,20},{8,24},{12,28},{16,0},{20,4},{24,8},{28,12},{1,17},{... | collective-permute-start | bytes 884744 | tf_op jit(solution)/shard_map/ppermute | solution.py:297
  681.9 58.2 %collective-permute-start.29 = (f32[96,768]{1,0:T(8,128)S(1)}, f32[96,768]{1,0:T(8,128)S(1)}, u32[]{:S(2)}, u32[]{:S(2)}) collective-permute-start(f32[96,768]{1,0:T(8,128)S(1)} %dynamic-slice_bitcast_fusion.2), channel_id=1, source_target_pairs={{0,16},{4,20},{8,24},{12,28},{16,0},{20,4},{24,8},{28,12},{1,17},{... | collective-permute-start | bytes 884744 | tf_op jit(solution)/shard_map/ppermute | solution.py:297
  697.3 49.1 %collective-permute-start.24 = (f32[96,768]{1,0:T(8,128)S(1)}, f32[96,768]{1,0:T(8,128)S(1)}, u32[]{:S(2)}, u32[]{:S(2)}) collective-permute-start(f32[96,768]{1,0:T(8,128)S(1)} %dynamic-slice_bitcast_fusion.3), channel_id=1, source_target_pairs={{0,16},{4,20},{8,24},{12,28},{16,0},{20,4},{24,8},{28,12},{1,17},{... | collective-permute-start | bytes 884744 | tf_op jit(solution)/shard_map/ppermute | solution.py:297
  702.2 50.6 %collective-permute-start.9 = (f32[96,768]{1,0:T(8,128)S(1)}, f32[96,768]{1,0:T(8,128)S(1)}, u32[]{:S(2)}, u32[]{:S(2)}) collective-permute-start(f32[96,768]{1,0:T(8,128)S(1)} %dynamic-slice_bitcast_fusion.4), channel_id=1, source_target_pairs={{0,16},{4,20},{8,24},{12,28},{16,0},{20,4},{24,8},{28,12},{1,17},{... | collective-permute-start | bytes 884744 | tf_op jit(solution)/shard_map/ppermute | solution.py:297
  730.7 26.4 %collective-permute-start.4 = (f32[96,768]{1,0:T(8,128)S(1)}, f32[96,768]{1,0:T(8,128)S(1)}, u32[]{:S(2)}, u32[]{:S(2)}) collective-permute-start(f32[96,768]{1,0:T(8,128)S(1)} %dynamic-slice_bitcast_fusion.5), channel_id=1, source_target_pairs={{0,16},{4,20},{8,24},{12,28},{16,0},{20,4},{24,8},{28,12},{1,17},{... | collective-permute-start | bytes 884744 | tf_op jit(solution)/shard_map/ppermute | solution.py:297
  753.5 52.1 %copy-start.92 = (f32[2,192,96]{1,2,0:T(8,128)S(1)}, f32[2,192,96]{1,2,0:T(8,128)}, u32[]{:S(2)}) copy-start(f32[2,192,96]{1,2,0:T(8,128)} %copy-done.91) | copy-start | bytes 442372
  (204 other events, 850.4 us)
